TPU v7x, 128 devices: a whole 4x4x4 slice. The times are simulated.
128 devices in a mesh: side: 2 (over z_lo), grp: 32 (over x, y, core), tp: 2 (over z_hi).
Axes of the slice: x: 4, y: 4, z: 4 (z_hi: 2, z_lo: 2; z = z_hi * 2 + z_lo), core: 2. Of those that a mesh axis runs over, the one named last changes fastest.
Arguments:
- query: bfloat16 [2, 256, 8192], P(None, 'grp', ('side', 'tp'))
- cache: bfloat16 [2, 256, 2, 4, 1024, 128], P(None, 'grp', None, ('side', 'tp'))
- cache_len: int32 [2, 256], P(None, 'grp'), may hold values from 1 to 1024, 131072 in all within a row
- row_slot: int32 [2, 256], replicated, may hold values from 0 to 255, each once within a row
- resid: bfloat16 [2, 256, 8192], P(None, None, 'grp')
- w_out: bfloat16 [8192, 8192], P(('side', 'tp'), 'grp'), may hold values from -0.5 to 0.5
- norm_gain: float32 [8192], P('grp'), may hold values from 0.1 to 1.9
- w_gate_up: bfloat16 [8192, 2, 32768], P(None, None, ('side', 'grp', 'tp')), may hold values from -0.25 to 0.25
- w_down: bfloat16 [32768, 8192], P(('side', 'grp', 'tp')), may hold values from -0.125 to 0.125
Outputs:
- layer_out: bfloat16 [2, 256, 8192], P(None, 'grp', ('side', 'tp'))
Inputs may be any that keep to these rules, and one draw needn't show every extreme that they name: `cache_len`: the lengths of one micro-batch sum to 131072, and one slot of each micro-batch holds exactly 1024. Each micro-batch's row_slot names every slot once.
All inputs are finite; a program needn't handle non-finite values. No bound on the sum of `cache_len` on one device may be relied on, other than what follows from the above.
Results may differ from a plain program's by a relative error of at most 0.0062.
Values may be sent and summed in bfloat16 or wider, within the bound.
A program may use at most 128 MiB of HBM per device.

v0:
```python
import math

import jax
import jax.numpy as jnp
from jax import lax
from jax.sharding import PartitionSpec as P

norm_epsilon = 1e-05


def slot_scores(queries, cached_keys):
    return jnp.einsum("rkgd,rkld->rkgl", queries, cached_keys, preferred_element_type=jnp.float32)


def shards(query, cache, cache_len, row_slot, resid, w_out, norm_gain, w_gate_up, w_down):
    micro_count = query.shape[0]
    slot_count = query.shape[1]
    kv_local = cache.shape[3]
    positions = cache.shape[4]
    head_size = cache.shape[5]
    group_heads = query.shape[2] // (kv_local * head_size)
    inv_root = 1.0 / math.sqrt(head_size)
    width_dev = w_out.shape[1]
    full_width = w_down.shape[1]
    hidden_dev = w_down.shape[0]
    group_index = lax.axis_index("grp")
    pair_index = lax.axis_index(("side", "tp"))
    gate_flat = w_gate_up.reshape(w_gate_up.shape[0], 2 * hidden_dev)
    position_ids = jnp.arange(positions)
    outputs = []
    for micro_index in range(micro_count):
        queries = query[micro_index].reshape(slot_count, kv_local, group_heads, head_size)
        cached_keys = cache[micro_index, :, 0]
        cached_values = cache[micro_index, :, 1]
        lengths = cache_len[micro_index]
        valid_mask = position_ids[None, None, None, :] < lengths[:, None, None, None]
        scores = slot_scores(queries, cached_keys) * inv_root
        scores = jnp.where(valid_mask, scores, -jnp.inf)
        weights = jax.nn.softmax(scores, axis=-1).astype(jnp.bfloat16)
        attended = jnp.einsum(
            "rkgl,rkld->rkgd", weights, cached_values, preferred_element_type=jnp.float32
        )
        attended = attended.astype(jnp.bfloat16).reshape(
            slot_count, kv_local * group_heads * head_size
        )
        by_slot = jnp.dot(
            lax.all_gather(attended, "grp", axis=0, tiled=True),
            w_out,
            preferred_element_type=jnp.float32,
        )
        projected = jnp.take(by_slot, row_slot[micro_index], axis=0)
        total_rows = projected.shape[0]
        residual_rows = resid[micro_index].astype(jnp.float32)
        mixed = residual_rows + lax.psum(projected, ("side", "tp"))
        squares = lax.psum(jnp.sum(mixed * mixed, axis=1), "grp")
        row_scale = lax.rsqrt(squares / full_width + norm_epsilon)
        normed = (mixed * row_scale[:, None] * norm_gain[None, :]).astype(jnp.bfloat16)
        residual_term = mixed * (pair_index == 0).astype(jnp.float32)
        gate_up = jnp.dot(
            lax.all_gather(normed, "grp", axis=1, tiled=True),
            gate_flat,
            preferred_element_type=jnp.float32,
        )
        gate_up = gate_up.reshape(total_rows, 2, hidden_dev)
        hidden = (jax.nn.silu(gate_up[:, 0]) * gate_up[:, 1]).astype(jnp.bfloat16)
        column_start = group_index * width_dev
        partial_value = jnp.dot(hidden, w_down, preferred_element_type=jnp.float32)
        current = lax.dynamic_slice_in_dim(partial_value, column_start, width_dev, 1)
        partial_rows = lax.psum_scatter(
            lax.dynamic_update_slice_in_dim(
                partial_value, current + residual_term, column_start, 1
            ),
            "grp",
            scatter_dimension=0,
            tiled=True,
        )
        result = lax.psum_scatter(partial_rows, ("side", "tp"), scatter_dimension=1, tiled=True)
        outputs.append(result.astype(jnp.bfloat16))
    return jnp.stack(outputs)


def solution(mesh):
    placed = (
        P(None, "grp", ("side", "tp")),
        P(None, "grp", None, ("side", "tp"), None, None),
        P(None, "grp"),
        P(),
        P(None, None, "grp"),
        P(("side", "tp"), "grp"),
        P("grp"),
        P(None, None, ("side", "grp", "tp")),
        P(("side", "grp", "tp"), None),
    )
    return jax.shard_map(
        shards,
        mesh=mesh,
        in_specs=placed,
        out_specs=P(None, "grp", ("side", "tp")),
        check_vma=False,
    )
```

profile of v0, /device:TPU:0, one launch (start us, length us, event | category | flops | bytes accessed | tf_op | source)
XLA Modules:
  0.0 569.8 jit_solution(10909815200855459512)
XLA Ops:
  8.2 2.4 fusion.66
  10.6 2.0 fusion.40
  13.4 2.5 fusion.65
  15.9 2.1 fusion.43
  18.7 39.9 %all-gather.9.cloned.1.call-done = bf16[256,2048]{1,0:T(8,128)(2,1)} async-done(((bf16[8,2048]{1,0:T(8,128)(2,1)}), bf16[256,2048]{1,0:T(8,128)(2,1)}) %all-gather.9.cloned.1.call-update) | async-done | bytes 1048592 | tf_op jit(solution)/shard_map/all_gather | solution.py:47
  58.6 1.7 fusion.76
  62.0 40.8 %all-gather.5.cloned.1.call-done = bf16[256,2048]{1,0:T(8,128)(2,1)} async-done(((bf16[8,2048]{1,0:T(8,128)(2,1)}), bf16[256,2048]{1,0:T(8,128)(2,1)}) %all-gather.5.cloned.1.call-update) | async-done | bytes 1048592 | tf_op jit(solution)/shard_map/all_gather | solution.py:47
  102.9 1.7 fusion.75
  106.4 42.8 %all-reduce.4.cloned.1.call-done = (f32[256,256]{1,0:T(8,128)}, f32[256,256]{1,0:T(8,128)}) async-done(((f32[256,256]{1,0:T(8,128)}, f32[256,256]{1,0:T(8,128)}), (f32[256,256]{1,0:T(8,128)}, f32[256,256]{1,0:T(8,128)})) %all-reduce.4.cloned.1.call-update) | async-done | bytes 524304 | tf_op jit(solution)/shard_map/psum | solution.py:54
  150.4 65.0 %all-reduce = (f32[256]{0:T(256)S(1)}, f32[256]{0:T(256)S(1)}) all-reduce(f32[256]{0:T(256)S(1)} %get-tuple-element.7, f32[256]{0:T(256)S(1)} %get-tuple-element.6), channel_id=1, replica_groups=mesh['side'=2,'grp'=32,'tp'=2] {'grp'}, use_global_device_ids=true, to_apply=%region_11.13 | all-reduce | flops 512 | bytes 4096 | tf_op jit(solution)/shard_map/psum | solution.py:55
  215.4 1.9 multiply_convert_fusion.1
  218.1 8.0 %copy.21 = bf16[1024,8,2,256]{3,1,2,0:T(8,128)(2,1)} copy(bf16[1024,8,2,256]{3,2,1,0:T(2,128)(2,1)} %bitcast.138) | data formatting | bytes 16777216
  226.2 11.8 %copy.12 = bf16[512,8192]{1,0:T(8,128)(2,1)} copy(bf16[512,8192]{0,1:T(8,128)(2,1)} %bitcast.137) | data formatting | bytes 16777216 | tf_op jit(solution)/shard_map/dot_general | solution.py:59
  238.0 24.1 %all-gather.7.cloned.1.call-done = bf16[256,8192]{1,0:T(8,128)(2,1)} async-done(((bf16[256,256]{1,0:T(8,128)(2,1)}), bf16[256,8192]{1,0:T(8,128)(2,1)}) %all-gather.7.cloned.1.call-update) | async-done | bytes 4194320 | tf_op jit(solution)/shard_map/all_gather | solution.py:60
  262.1 7.2 %fusion.4 = f32[256,2,256]{2,0,1:T(8,128)S(1)} fusion(bf16[2,256,8192]{2,1,0:T(8,128)(2,1)} %bitcast.139, bf16[256,8192]{1,0:T(8,128)(2,1)} %all-gather.7.cloned.1.call-done), kind=kOutput, calls=%fused_computation.6 | convolution fusion | flops 2147483648 | bytes 13107200 | tf_op jit(solution)/shard_map/dot_general | solution.py:59
  269.3 4.5 fusion.52
  273.8 39.1 %all-gather.11.cloned.1.call-done = bf16[256,8192]{1,0:T(8,128)(2,1)} async-done(((bf16[256,256]{1,0:T(8,128)(2,1)}), bf16[256,8192]{1,0:T(8,128)(2,1)}) %all-gather.11.cloned.1.call-update) | async-done | bytes 4194320 | tf_op jit(solution)/shard_map/all_gather | solution.py:60
  312.8 7.2 %fusion.2 = f32[256,2,256]{2,0,1:T(8,128)S(1)} fusion(bf16[2,256,8192]{2,1,0:T(8,128)(2,1)} %bitcast.140, bf16[256,8192]{1,0:T(8,128)(2,1)} %all-gather.11.cloned.1.call-done), kind=kOutput, calls=%fused_computation.4 | convolution fusion | flops 2147483648 | bytes 13107200 | tf_op jit(solution)/shard_map/dot_general | solution.py:59
  320.0 4.5 fusion.54
  324.5 1.9 add_dynamic-update-slice_fusion.1
  327.3 91.5 %reduce-scatter.5.cloned.1.call-done = f32[8,8192]{1,0:T(8,128)} async-done(((f32[256,8192]{1,0:T(8,128)}), f32[8,8192]{1,0:T(8,128)}) %reduce-scatter.5.cloned.1.call-update) | async-done | bytes 262160 | tf_op jit(solution)/shard_map/reduce_scatter | solution.py:69
  418.9 96.1 %reduce-scatter.9.cloned.1.call-done = f32[8,8192]{1,0:T(8,128)} async-done(((f32[256,8192]{1,0:T(8,128)}), f32[8,8192]{1,0:T(8,128)}) %reduce-scatter.9.cloned.1.call-update) | async-done | bytes 262160 | tf_op jit(solution)/shard_map/reduce_scatter | solution.py:69
  515.0 23.6 %reduce-scatter.7.cloned.1.call-done = f32[8,2048]{1,0:T(8,128)} async-done(((f32[8,8192]{1,0:T(8,128)}), f32[8,2048]{1,0:T(8,128)}) %reduce-scatter.7.cloned.1.call-update) | async-done | bytes 65552 | tf_op jit(solution)/shard_map/reduce_scatter | solution.py:77
  539.5 22.4 %reduce-scatter.11.cloned.1.call-done = f32[8,2048]{1,0:T(8,128)} async-done(((f32[8,8192]{1,0:T(8,128)}), f32[8,2048]{1,0:T(8,128)}) %reduce-scatter.11.cloned.1.call-update) | async-done | bytes 65552 | tf_op jit(solution)/shard_map/reduce_scatter | solution.py:77
  (57 shorter events, 11.9 us)
Async XLA Ops:
  6.5 52.1 %copy-start = (bf16[2048,256]{1,0:T(8,128)(2,1)S(1)}, bf16[2048,256]{1,0:T(8,128)(2,1)}, u32[]{:S(2)}) copy-start(bf16[2048,256]{1,0:T(8,128)(2,1)} %param.16) | copy-start | bytes 3145732
  6.5 12.1 %copy-start.7 = (s32[2,256]{1,0:T(2,128)S(1)}, s32[2,256]{1,0:T(2,128)}, u32[]{:S(2)}) copy-start(s32[2,256]{1,0:T(2,128)} %param.14) | copy-start | bytes 6148
  6.5 52.0 %all-gather.9.cloned.1.call-start = ((), (), s32[]{:S(2)}) async-start(), calls=%async_computation.8 | async-start | bytes 1081344 | tf_op jit(solution)/shard_map/all_gather | solution.py:47
  13.3 89.6 %all-gather.5.cloned.1.call-start = ((), (), s32[]{:S(2)}) async-start(), calls=%async_computation.4 | async-start | bytes 1081344 | tf_op jit(solution)/shard_map/all_gather | solution.py:47
  13.4 135.8 %copy-start.4 = (bf16[2,256,256]{2,1,0:T(8,128)(2,1)S(1)}, bf16[2,256,256]{2,1,0:T(8,128)(2,1)}, u32[]{:S(2)}) copy-start(bf16[2,256,256]{2,1,0:T(8,128)(2,1)} %param.15) | copy-start | bytes 786436
  15.9 199.5 %copy-start.8 = (f32[256]{0:T(256)S(1)}, f32[256]{0:T(256)}, u32[]{:S(2)}) copy-start(f32[256]{0:T(256)} %param.17) | copy-start | bytes 3076
  18.6 130.6 %all-reduce.4.cloned.1.call-start = ((), (), s32[]{:S(2)}) async-start(), calls=%async_computation.12 | async-start | bytes 1048576 | tf_op jit(solution)/shard_map/psum | solution.py:54
  106.3 155.7 %all-gather.7.cloned.1.call-start = ((), (), s32[]{:S(2)}) async-start(), calls=%async_computation.5 | async-start | bytes 4325376 | tf_op jit(solution)/shard_map/all_gather | solution.py:60
  217.3 95.5 %all-gather.11.cloned.1.call-start = ((), (), s32[]{:S(2)}) async-start(), calls=%async_computation.9 | async-start | bytes 4325376 | tf_op jit(solution)/shard_map/all_gather | solution.py:60
  217.9 200.9 %reduce-scatter.5.cloned.1.call-start = ((), (), s32[]{:S(2)}) async-start(), calls=%async_computation.6 | async-start | bytes 8650752 | tf_op jit(solution)/shard_map/reduce_scatter | solution.py:69
  262.1 7.2 %copy-start.2 = (bf16[256,8192]{1,0:T(8,128)(2,1)S(1)}, bf16[256,8192]{1,0:T(8,128)(2,1)}, u32[]{:S(2)}) copy-start(bf16[256,8192]{1,0:T(8,128)(2,1)} %param.19) | copy-start | bytes 12582916
  312.8 7.2 %copy-start.3 = (bf16[256,8192]{1,0:T(8,128)(2,1)S(1)}, bf16[256,8192]{1,0:T(8,128)(2,1)}, u32[]{:S(2)}) copy-start(bf16[256,8192]{1,0:T(8,128)(2,1)} %param.19) | copy-start | bytes 12582916
  320.0 4.5 copy-start.5
  320.0 4.5 copy-start.6
  326.5 236.8 %copy-start.1 = (bf16[2048,256]{1,0:T(8,128)(2,1)S(1)}, bf16[2048,256]{1,0:T(8,128)(2,1)}, u32[]{:S(2)}) copy-start(bf16[2048,256]{1,0:T(8,128)(2,1)} %param.16) | copy-start | bytes 3145732
  326.5 188.5 %reduce-scatter.9.cloned.1.call-start = ((), (), s32[]{:S(2)}) async-start(), calls=%async_computation.10 | async-start | bytes 8650752 | tf_op jit(solution)/shard_map/reduce_scatter | solution.py:69
  327.3 211.3 %reduce-scatter.7.cloned.1.call-start = ((), (), s32[]{:S(2)}) async-start(), calls=%async_computation.7 | async-start | bytes 327680 | tf_op jit(solution)/shard_map/reduce_scatter | solution.py:77
  418.8 143.0 %reduce-scatter.11.cloned.1.call-start = ((), (), s32[]{:S(2)}) async-start(), calls=%async_computation.11 | async-start | bytes 327680 | tf_op jit(solution)/shard_map/reduce_scatter | solution.py:77
Sparse Core Ops, SparseCore 0:
  13.5 45.0 all-gather.8
  60.8 41.9 all-gather.4
  106.5 42.6 all-reduce.3
  217.4 44.6 all-gather.6
  264.1 48.6 all-gather.10
  326.6 92.1 reduce-scatter.4
  423.0 91.9 reduce-scatter.8
  517.3 21.2 reduce-scatter.6
  541.1 20.6 reduce-scatter.10
where the time goes:
time: 571 us; the launch traced here: 570 us
  waiting for transfers between devices  422 us (74%)
  blocking collectives  65 us (11%)
  matrix products  35.7 us (6%)
  local copies, waits for them, and re-layouts  24.7 us (4%)
  between operations  13.4 us (2%)
  other arithmetic  9.09 us (2%)
    reduce_scatter x2, waiting for transfers between devices, shards(): lax.psum_scatter(lax.dynamic_update_slice_in_dim(partial_value, current +...  188 us
    all_gather x2, waiting for transfers between devices, shards(): lax.all_gather(attended, 'grp', axis=0, tiled=True)  80.7 us
    psum x1, blocking collectives, shards(): squares = lax.psum(jnp.sum(mixed * mixed, axis=1), 'grp')  65 us
    all_gather x2, waiting for transfers between devices, shards(): lax.all_gather(normed, 'grp', axis=1, tiled=True)  63.2 us
    reduce_scatter x2, waiting for transfers between devices, shards(): lax.psum_scatter(partial_rows, ('side', 'tp'), scatter_dimension=1, tiled...  46 us
    psum x1, waiting for transfers between devices, shards(): mixed = residual_rows + lax.psum(projected, ('side', 'tp'))  42.8 us
    dot_general x2, matrix products, shards(): jnp.dot(lax.all_gather(normed, 'grp', axis=1, tiled=True), gate_flat, pre...  14.3 us
    dot_general x1, local copies, waits for them, and re-layouts, shards(): jnp.dot(lax.all_gather(normed, 'grp', axis=1, tiled=True), gate_flat, pre...  11.8 us
  transfers between devices with their start and end apart: 9, of which 9 were waited for; matrix products, arithmetic and copies ran while one was open for 7% of the time, Pallas kernels for 0%

commit v1 on v0

v1 whole, which is shorter than its diff:
```python
import math

import jax
import jax.numpy as jnp
from jax import lax
from jax.experimental import pallas as pl
from jax.experimental.pallas import tpu as pltpu
from jax.sharding import PartitionSpec as P

MESH = pl.DeviceIdType.MESH
F32 = jnp.float32
BF16 = jnp.bfloat16
EPS = 1e-05
N = 4
COLS = (640, 640, 768)
STARTS = (0, 640, 1280)
GATHER_PARTS = ((0, 32, 0, 384), (32, 32, 0, 384), (0, 64, 384, 128))
ORDERS = ((0, 1, 2), (1, 2, 0), (2, 0, 1))
W_CHUNKS = 8


def column_shard(z):
    return lax.rem(z, 2) * 2 + z // 2


def static_column_shard(z):
    return (z % 2) * 2 + z // 2


def dot(a, b):
    return jnp.dot(a, b, preferred_element_type=F32)


def layer_kernel(
    att_ref, rows_ref, owned_ref, resid_ref, wo_ref, gain_ref, wg_ref, wd_ref,
    out_ref,
    att_all, wo_all, resid_all, gain_all, w_raw, w_all, wd_all,
    proj_send, proj_recv, gathered, stats, acc, hid, pick, pick_sib,
    sums0, sums1, sums2, in10, in11, in12, t10, t11, t12,
    in20, in21, in22, t20, t21, t22, in30, in31, in32,
    res_own, res_send, res_recv,
    local_sem, sib_send, sib_recv, a_send, a_recv, b_send, b_recv,
    g_send, g_recv, s_send, s_recv, r_send, r_recv,
):
    g = lax.axis_index("grp")
    side = lax.axis_index("side")
    tp = lax.axis_index("tp")
    core = lax.rem(g, 2)
    y = lax.rem(g // 2, N)
    x = g // 8
    z = tp * 2 + side
    here = (x, y, z)
    xy = x * N + y

    def device(cx, cy, cz, cc):
        return {"side": lax.rem(cz, 2), "grp": (cx * N + cy) * 2 + cc, "tp": cz // 2}

    def along(axis, k):
        moved = list(here)
        moved[axis] = lax.rem(here[axis] + k, N)
        return moved[axis], device(moved[0], moved[1], moved[2], core)

    sibling = device(x, y, z, 1 - core)

    def remote(src, dst, send, recv, target):
        copy = pltpu.make_async_remote_copy(
            src_ref=src, dst_ref=dst, send_sem=send, recv_sem=recv,
            device_id=target, device_id_type=MESH,
        )
        copy.start()
        return copy

    def local(src, dst, sem):
        copy = pltpu.make_async_copy(src, dst, sem)
        copy.start()
        return copy

    barrier = pltpu.get_barrier_semaphore()
    for axis in range(3):
        for k in (1, 2, 3):
            pl.semaphore_signal(barrier, inc=1, device_id=along(axis, k)[1], device_id_type=MESH)
    pl.semaphore_signal(barrier, inc=1, device_id=sibling, device_id_type=MESH)
    raw_rows = w_raw.shape[0] // W_CHUNKS
    raw_loads = [
        local(wg_ref.at[pl.ds(i * raw_rows, raw_rows)], w_raw.at[pl.ds(i * raw_rows, raw_rows)], local_sem.at[i])
        for i in range(W_CHUNKS)
    ]
    own_loads = [
        local(wo_ref, wo_all.at[core], local_sem.at[W_CHUNKS]),
        local(resid_ref, resid_all.at[core], local_sem.at[W_CHUNKS + 1]),
        local(wd_ref, wd_all.at[core], local_sem.at[W_CHUNKS + 2]),
    ]
    att_all[x, y] = att_ref[...]
    gain_all[core] = gain_ref[...]
    pl.semaphore_wait(barrier, 10)

    half = att_all.shape[3] // 2
    first = []
    for part, axis in ((0, 0), (1, 1)):
        cols = pl.ds(part * half, half)
        for k in (1, 2, 3):
            ref = att_all.at[x, y, :, cols]
            first.append(remote(ref, ref, a_send.at[0, part, k - 1], a_recv.at[0, part, k - 1], along(axis, k)[1]))
    exchange = [
        remote(wo_ref, wo_all.at[core], sib_send.at[0], sib_recv.at[0], sibling),
        remote(resid_ref, resid_all.at[core], sib_send.at[1], sib_recv.at[1], sibling),
        remote(gain_ref, gain_all.at[core], sib_send.at[2], sib_recv.at[2], sibling),
        remote(wd_ref, wd_all.at[core], sib_send.at[3], sib_recv.at[3], sibling),
    ]

    p_out = lax.broadcasted_iota(jnp.int32, (256, 256), 0)
    p_in = lax.broadcasted_iota(jnp.int32, (256, 256), 1)
    order = jnp.where(p_in == (p_out % 64) * 4 + p_out // 64, 1.0, 0.0).astype(BF16)

    def untangle(chunk):
        raw_loads[chunk].wait()
        span = w_raw.shape[0] // (W_CHUNKS * 512)

        def step(u, _):
            unit = chunk * span + u
            row = pl.multiple_of(unit * 512, 512)
            both = jnp.concatenate([w_raw[pl.ds(row, 256)], w_raw[pl.ds(row + 256, 256)]], axis=1)
            apart = dot(order, both).astype(BF16)
            base = pl.multiple_of(unit * 128, 128)
            for l in range(2):
                for c in range(2):
                    rows = slice((l * 2 + c) * 64, (l * 2 + c) * 64 + 64)
                    lanes = pl.ds(c * 256 + l * 128, 128)
                    w_all[core, pl.ds(base, 64), lanes] = apart[rows, 0:128]
                    w_all[core, pl.ds(base + 64, 64), lanes] = apart[rows, 128:256]
            return 0

        lax.fori_loop(0, span, step, 0)
        block = w_all.at[core, pl.ds(chunk * span * 128, span * 128)]
        exchange.append(remote(block, block, sib_send.at[4 + chunk], sib_recv.at[4 + chunk], sibling))

    def slot_of(r, parity):
        return ((r // 16) * 2 + parity) * 8 + r % 8

    def choose(parity_slots, parity_rows):
        r = lax.broadcasted_iota(jnp.int32, (256, 256), 0)
        o = lax.broadcasted_iota(jnp.int32, (256, 256), 1)
        same = (r % 16) // 8 == (o % 16) // 8
        hit = same & (slot_of(r, parity_slots) == owned_ref[pl.ds(parity_rows, 1), :])
        return jnp.transpose(jnp.where(hit, 1.0, 0.0)).astype(BF16)

    for chunk in range(0, 3):
        untangle(chunk)
    for copy in first:
        copy.wait_recv()
    second = []
    for part, axis in ((0, 1), (1, 0)):
        cols = pl.ds(part * half, half)
        for k in (1, 2, 3):
            ref = att_all.at[:, y, :, cols] if part == 0 else att_all.at[x, :, :, cols]
            second.append(remote(ref, ref, a_send.at[1, part, k - 1], a_recv.at[1, part, k - 1], along(axis, k)[1]))
    for chunk in range(3, W_CHUNKS):
        untangle(chunk)
    own_loads[0].wait()
    exchange[0].wait_recv()
    for copy in second:
        copy.wait_recv()

    rows_all = att_all[...].reshape(256, 2 * half)
    for c in range(2):
        proj_send[:, :, c * 256:(c + 1) * 256] = dot(rows_all, wo_all[c]).astype(BF16).reshape(N, 64, 256)
    sends = []
    for k in (1, 2, 3):
        there, target = along(2, k)
        sends.append(remote(proj_send.at[there], proj_recv.at[k - 1], b_send.at[k - 1], b_recv.at[k - 1], target))

    own_loads[1].wait()
    exchange[1].wait_recv()
    exchange[2].wait_recv()
    r = z * 64 + lax.broadcasted_iota(jnp.int32, (64, 512), 0)
    o = lax.broadcasted_iota(jnp.int32, (64, 512), 1)
    hit = ((r % 16) // 8 == o // 256) & (slot_of(r, core) == rows_ref[...])
    served = jnp.where(hit, 1.0, 0.0).astype(BF16)
    resid_rows = jnp.concatenate([dot(served, resid_all[0]), dot(served, resid_all[1])], axis=1)
    gain_row = jnp.concatenate(
        [gain_all[0, 0:1], gain_all[0, 1:2], gain_all[1, 0:1], gain_all[1, 1:2]], axis=1
    )
    for copy in sends:
        copy.wait_recv()
    mixed = resid_rows + (
        (proj_send[z].astype(F32) + proj_recv[0].astype(F32))
        + (proj_recv[1].astype(F32) + proj_recv[2].astype(F32))
    )
    gathered[x, y, z] = (mixed * gain_row).astype(BF16)
    squares = jnp.sum(mixed * mixed, axis=1, keepdims=True)
    tall = jnp.concatenate([jnp.broadcast_to(squares, (64, 128)), jnp.zeros((64, 128), F32)], axis=0)
    stats[x, y, z, 0:4] = jnp.transpose(tall)[0:4]
    stats[x, y, z, 4:6] = gain_all[0, 0:2]
    stats[x, y, z, 6:8] = gain_all[1, 0:2]

    def gather_phase(phase):
        started = []
        for part, (row, rows, col, cols) in enumerate(GATHER_PARTS):
            axes = ORDERS[part]
            index = list(here)
            for done in axes[:phase]:
                index[done] = slice(None)
            block = gathered.at[index[0], index[1], index[2], pl.ds(row, rows), pl.ds(col, cols)]
            for k in (1, 2, 3):
                target = along(axes[phase], k)[1]
                started.append(remote(block, block, g_send.at[phase, part, k - 1], g_recv.at[phase, part, k - 1], target))
                if part == 2:
                    tile = stats.at[index[0], index[1], index[2]]
                    started.append(remote(tile, tile, s_send.at[phase, k - 1], s_recv.at[phase, k - 1], target))
        return started

    gathers = []
    for phase in range(3):
        now = gather_phase(phase)
        if phase == 0:
            for parity in range(2):
                pick[parity] = choose(parity, core)
            pick_sib[...] = choose(core, 1 - core)
        for copy in now:
            copy.wait_recv()
        gathers += now

    for chunk in range(W_CHUNKS):
        exchange[4 + chunk].wait_recv()
    acc[...] = jnp.zeros_like(acc)

    def multiply(i, _):
        block = gathered[i // N, lax.rem(i, N)].reshape(256, 512)
        row = pl.multiple_of(i * 512, 512)
        for p in range(2):
            acc[:, p * 512:(p + 1) * 512] += dot(block, w_all[p, pl.ds(row, 512), :])
        return 0

    lax.fori_loop(0, 16, multiply, 0)
    columns = []
    total = jnp.sum(stats[...].reshape(16, N, 8, 128), axis=0)
    for zz in range(N):
        spread = jnp.transpose(jnp.broadcast_to(total[zz, 0:1], (128, 128)))
        columns.append(spread[0:64])
    row_scale = lax.rsqrt(jnp.concatenate(columns, axis=0) * (1.0 / 8192) + EPS)
    row_scale = jnp.concatenate([row_scale, row_scale], axis=1)
    for p in range(2):
        gate = acc[:, p * 512:p * 512 + 256] * row_scale
        up = acc[:, p * 512 + 256:p * 512 + 512] * row_scale
        hid[core, :, p * 256:(p + 1) * 256] = (gate / (1.0 + jnp.exp(-gate)) * up).astype(BF16)
    hid_copy = remote(hid.at[core], hid.at[core], sib_send.at[12], sib_recv.at[12], sibling)
    own_loads[2].wait()
    exchange[3].wait_recv()

    shard = column_shard(z)
    mine = pick[core, pl.ds(pl.multiple_of(xy * 16, 16), 16), :]
    other = pick_sib[pl.ds(pl.multiple_of(xy * 16, 16), 16), :]
    for j in range(N):
        block = gathered[shard, j].reshape(256, 512)
        res_own[:, j * 512:(j + 1) * 512] = dot(mine, block)
        res_send[:, j * 512:(j + 1) * 512] = dot(other, block).astype(BF16)
    res_copy = remote(res_send, res_recv, sib_send.at[13], sib_recv.at[13], sibling)
    hid_copy.wait_recv()

    ours = (dot(pick[0], hid[0]) + dot(pick[1], hid[1])).astype(BF16)
    sums = (sums0, sums1, sums2)
    in1 = (in10, in11, in12)
    t1 = (t10, t11, t12)
    in2 = (in20, in21, in22)
    t2 = (t20, t21, t22)
    in3 = (in30, in31, in32)
    reduces = {}
    for part in range(3):
        for zz in range(N):
            lanes = pl.ds(static_column_shard(zz) * 2048 + STARTS[part], COLS[part])
            value = dot(ours[:, 0:256], wd_all[0, :, lanes]) + dot(ours[:, 256:512], wd_all[1, :, lanes])
            sums[part][:, :, zz] = value.astype(BF16).reshape(N, N, 16, COLS[part])
        axis = ORDERS[part][0]
        for k in (1, 2, 3):
            there, target = along(axis, k)
            index = [slice(None)] * 3
            index[axis] = there
            reduces[0, part, k] = remote(
                sums[part].at[index[0], index[1], index[2]], in1[part].at[k - 1],
                r_send.at[0, part, k - 1], r_recv.at[0, part, k - 1], target,
            )

    def add(own, incoming):
        return (own.astype(F32) + incoming[0].astype(F32)) + (incoming[1].astype(F32) + incoming[2].astype(F32))

    for part in range(3):
        for k in (1, 2, 3):
            reduces[0, part, k].wait_recv()
        axes = ORDERS[part]

        def fold(i, _, part=part, axes=axes):
            left = sorted(axes[1:])
            index = [None] * 3
            index[axes[0]] = here[axes[0]]
            index[left[0]] = i // N
            index[left[1]] = lax.rem(i, N)
            i0, i1 = i // N, lax.rem(i, N)
            own = sums[part][index[0], index[1], index[2]]
            t1[part][i0, i1] = add(own, [in1[part][q, i0, i1] for q in range(3)]).astype(BF16)
            return 0

        lax.fori_loop(0, 16, fold, 0)
        left = sorted(axes[1:])
        place = left.index(axes[1])
        for k in (1, 2, 3):
            there, target = along(axes[1], k)
            src = t1[part].at[there] if place == 0 else t1[part].at[:, there]
            reduces[1, part, k] = remote(
                src, in2[part].at[k - 1], r_send.at[1, part, k - 1], r_recv.at[1, part, k - 1], target
            )
    for part in range(3):
        for k in (1, 2, 3):
            reduces[1, part, k].wait_recv()
        axes = ORDERS[part]
        place = sorted(axes[1:]).index(axes[1])
        coord = here[axes[1]]
        for i in range(N):
            own = t1[part][coord, i] if place == 0 else t1[part][i, coord]
            t2[part][i] = add(own, [in2[part][q, i] for q in range(3)]).astype(BF16)
        for k in (1, 2, 3):
            there, target = along(axes[2], k)
            reduces[2, part, k] = remote(
                t2[part].at[there], in3[part].at[k - 1],
                r_send.at[2, part, k - 1], r_recv.at[2, part, k - 1], target,
            )
    res_copy.wait_recv()
    pieces = []
    for j in range(N):
        for q in range(4):
            pieces.append(stats[shard, j, z, 4 + q:5 + q])
    residual = (res_own[...] + res_recv[...].astype(F32)) / jnp.concatenate(pieces, axis=1)
    for part in range(3):
        for k in (1, 2, 3):
            reduces[2, part, k].wait_recv()
        own = t2[part][here[ORDERS[part][2]]]
        total = add(own, [in3[part][q] for q in range(3)])
        lanes = slice(STARTS[part], STARTS[part] + COLS[part])
        out_ref[:, lanes] = (residual[:, lanes] + total).astype(BF16)

    for copy in first + second + exchange + sends + gathers + [hid_copy, res_copy] + list(reduces.values()):
        copy.wait_send()


def attend(query, cache, cache_len):
    micro_count, slot_count = query.shape[0], query.shape[1]
    positions, head_size = cache.shape[4], cache.shape[5]
    heads = query.shape[2] // head_size
    position_ids = jnp.arange(positions)
    outputs = []
    for m in range(micro_count):
        queries = query[m].reshape(slot_count, 1, heads, head_size)
        scores = jnp.einsum("rkgd,rkld->rkgl", queries, cache[m, :, 0], preferred_element_type=F32)
        scores = scores * (1.0 / math.sqrt(head_size))
        live = position_ids[None, None, None, :] < cache_len[m][:, None, None, None]
        scores = jnp.where(live, scores, -jnp.inf)
        weights = jax.nn.softmax(scores, axis=-1).astype(BF16)
        attended = jnp.einsum("rkgl,rkld->rkgd", weights, cache[m, :, 1], preferred_element_type=F32)
        outputs.append(attended.astype(BF16).reshape(slot_count, heads * head_size))
    return jnp.concatenate(outputs, axis=0)


def shards(query, cache, cache_len, row_slot, resid, w_out, norm_gain, w_gate_up, w_down):
    attended = attend(query, cache, cache_len)
    rows = row_slot.reshape(1, 512)
    owned = row_slot.reshape(2, 16, 2, 8).transpose(2, 1, 0, 3).reshape(2, 256)
    gain = jnp.tile(norm_gain.reshape(2, 128), (4, 1))
    raw = w_gate_up.reshape(8192, 2, 2, 128).transpose(0, 2, 1, 3).reshape(32768, 128)
    vmem = pl.BlockSpec(memory_space=pltpu.VMEM)
    hbm = pl.BlockSpec(memory_space=pl.ANY)
    sem = pltpu.SemaphoreType.DMA
    scratch = [
        pltpu.VMEM((N, N, 16, 2048), BF16),
        pltpu.VMEM((2, 2048, 256), BF16),
        pltpu.VMEM((2, 512, 256), BF16),
        pltpu.VMEM((2, 8, 128), F32),
        pltpu.VMEM((32768, 128), BF16),
        pltpu.VMEM((2, 8192, 512), BF16),
        pltpu.VMEM((2, 256, 8192), BF16),
        pltpu.VMEM((N, 64, 512), BF16),
        pltpu.VMEM((3, 64, 512), BF16),
        pltpu.VMEM((N, N, N, 64, 512), BF16),
        pltpu.VMEM((N, N, N, 8, 128), F32),
        pltpu.VMEM((256, 1024), F32),
        pltpu.VMEM((2, 256, 512), BF16),
        pltpu.VMEM((2, 256, 256), BF16),
        pltpu.VMEM((256, 256), BF16),
    ]
    scratch += [pltpu.VMEM((N, N, N, 16, c), BF16) for c in COLS]
    scratch += [pltpu.VMEM((3, N, N, 16, c), BF16) for c in COLS]
    scratch += [pltpu.VMEM((N, N, 16, c), BF16) for c in COLS]
    scratch += [pltpu.VMEM((3, N, 16, c), BF16) for c in COLS]
    scratch += [pltpu.VMEM((N, 16, c), BF16) for c in COLS]
    scratch += [pltpu.VMEM((3, 16, c), BF16) for c in COLS]
    scratch += [
        pltpu.VMEM((16, 2048), F32),
        pltpu.VMEM((16, 2048), BF16),
        pltpu.VMEM((16, 2048), BF16),
    ]
    scratch += [
        sem((W_CHUNKS + 3,)),
        sem((14,)), sem((14,)),
        sem((2, 2, 3)), sem((2, 2, 3)),
        sem((3,)), sem((3,)),
        sem((3, 3, 3)), sem((3, 3, 3)),
        sem((3, 3)), sem((3, 3)),
        sem((3, 3, 3)), sem((3, 3, 3)),
    ]
    out = pl.pallas_call(
        layer_kernel,
        out_shape=jax.ShapeDtypeStruct((16, 2048), BF16),
        in_specs=[vmem, vmem, vmem, hbm, hbm, vmem, hbm, hbm],
        out_specs=vmem,
        scratch_shapes=scratch,
        compiler_params=pltpu.CompilerParams(
            collective_id=0, has_side_effects=True, vmem_limit_bytes=60 * 1024 * 1024
        ),
        name="layer",
    )(attended, rows, owned, resid.reshape(512, 256), w_out, gain, raw, w_down)
    return out.reshape(2, 8, 2048)


def solution(mesh):
    placed = (
        P(None, "grp", ("side", "tp")),
        P(None, "grp", None, ("side", "tp"), None, None),
        P(None, "grp"),
        P(),
        P(None, None, "grp"),
        P(("side", "tp"), "grp"),
        P("grp"),
        P(None, None, ("side", "grp", "tp")),
        P(("side", "grp", "tp"), None),
    )
    return jax.shard_map(
        shards,
        mesh=mesh,
        in_specs=placed,
        out_specs=P(None, "grp", ("side", "tp")),
        check_vma=False,
    )
```

time: 571 us -> 113 us (0.20)
  waiting for transfers between devices: 422 us -> 0 us
  Pallas kernels: 0 us -> 98.3 us
  blocking collectives: 65 us -> 0 us
  matrix products: 35.7 us -> 8.92 us
  local copies, waits for them, and re-layouts: 24.7 us -> 5.06 us
  between operations: 13.4 us -> 0.05 us
  other arithmetic: 9.09 us -> 0.72 us
    reduce_scatter x4 -> x0, waiting for transfers between devices: 234 us -> none  [the longest x2 188 us: shards(): lax.psum_scatter(lax.dynamic_update_slice_in_dim(partial_value, current +...]
    all_gather x4 -> x0, waiting for transfers between devices: 144 us -> none  [the longest x2 80.7 us: shards(): lax.all_gather(attended, 'grp', axis=0, tiled=True)]
    pallas_call x0 -> x1, Pallas kernels: none -> 98.3 us  [shards(): pl.pallas_call(layer_kernel, out_shape=jax.ShapeDtypeStruct((16, 2048), B...]
    psum x1 -> x0, blocking collectives: 65 us -> none  [shards(): squares = lax.psum(jnp.sum(mixed * mixed, axis=1), 'grp')]
    psum x1 -> x0, waiting for transfers between devices: 42.8 us -> none  [shards(): mixed = residual_rows + lax.psum(projected, ('side', 'tp'))]
    dot_general x8 -> x2, matrix products: 30.8 us -> 4.08 us  [attend(): jnp.einsum('rkgl,rkld->rkgd', weights, cache[m, :, 1], preferred_element_...]
    dot_general x1 -> x0, local copies, waits for them, and re-layouts: 11.8 us -> none  [shards(): jnp.dot(lax.all_gather(normed, 'grp', axis=1, tiled=True), gate_flat, pre...]
    unnamed x22 -> x9, local copies, waits for them, and re-layouts: 10.1 us -> 2.88 us
  transfers between devices with their start and end apart: 9 -> 0, of which waited for: 9 -> 0; matrix products, arithmetic and copies ran while one was open for 7% -> 0% of each run, Pallas kernels for 0% -> 0%
where the time goes in v1:
time: 113 us
  Pallas kernels  98.3 us (87%)
  matrix products  8.92 us (8%)
  local copies, waits for them, and re-layouts  5.06 us (4%)
    pallas_call x1, Pallas kernels, shards(): pl.pallas_call(layer_kernel, out_shape=jax.ShapeDtypeStruct((16, 2048), B...  98.3 us
    sub x2, matrix products, attend(): weights = jax.nn.softmax(scores, axis=-1).astype(BF16)  4.84 us
    dot_general x2, matrix products, attend(): jnp.einsum('rkgl,rkld->rkgd', weights, cache[m, :, 1], preferred_element_...  4.08 us
    unnamed x9, local copies, waits for them, and re-layouts  2.88 us

profile of v1, /device:TPU:0, one launch (start us, length us, event | category | flops | bytes accessed | tf_op | source)
XLA Modules:
  0.0 113.1 jit_solution(1709589621630132126)
XLA Ops:
  0.0 0.0 copy-start
  0.0 0.0 copy-start.1
  0.0 0.8 slice_bitcast_fusion.3
  0.8 0.1 iota_compare_fusion
  0.8 0.8 slice_bitcast_fusion.1
  1.6 2.4 %fusion.49 = (f32[8,16]{1,0:T(8,128)S(1)}, f32[8,16,1024]{2,1,0:T(8,128)S(1)}) fusion(bf16[2,8,2,1,1024,128]{5,4,3,2,1,0:T(8,128)(2,1)} %param.10, pred[8,1024]{1,0:T(8,128)(4,1)S(1)} %get-tuple-element.14, bf16[1,8,16,128]{3,1,2,0:T(8,128)(2,1)S(1)} %get-tuple-element.5), kind=kOutput, calls=%fused_computation.44 | convolution fusion | flops 34079744 | bytes 2662912 | tf_op jit(solution)/shard_map/sub | solution.py:356
  4.0 2.0 %fusion.39 = bf16[1,8,16,128]{3,2,1,0:T(8,128)(2,1)S(1)} fusion(bf16[2,8,2,1,1024,128]{5,4,3,2,1,0:T(8,128)(2,1)} %param.10, f32[8,16,1024]{2,1,0:T(8,128)S(1)} %get-tuple-element.12, f32[8,16]{1,0:T(8,128)S(1)} %get-tuple-element.11), kind=kOutput, calls=%fused_computation.25 | convolution fusion | flops 33832960 | bytes 2654720 | tf_op jit(solution)/shard_map/rkgl,rkld->rkgd/dot_general | solution.py:357
  6.1 2.4 %fusion.48 = (f32[8,16]{1,0:T(8,128)S(1)}, f32[8,16,1024]{2,1,0:T(8,128)S(1)}) fusion(bf16[2,8,2,1,1024,128]{5,4,3,2,1,0:T(8,128)(2,1)} %param.10, pred[8,1024]{1,0:T(8,128)(4,1)S(1)} %get-tuple-element.13, bf16[1,8,16,128]{3,1,2,0:T(8,128)(2,1)S(1)} %get-tuple-element.6), kind=kOutput, calls=%fused_computation.43 | convolution fusion | flops 34079744 | bytes 2662912 | tf_op jit(solution)/shard_map/sub | solution.py:356
  8.5 2.0 %fusion.36 = bf16[1,8,16,128]{3,2,1,0:T(8,128)(2,1)S(1)} fusion(bf16[2,8,2,1,1024,128]{5,4,3,2,1,0:T(8,128)(2,1)} %param.10, f32[8,16,1024]{2,1,0:T(8,128)S(1)} %get-tuple-element.10, f32[8,16]{1,0:T(8,128)S(1)} %get-tuple-element.9), kind=kOutput, calls=%fused_computation.24 | convolution fusion | flops 33832960 | bytes 2654720 | tf_op jit(solution)/shard_map/rkgl,rkld->rkgd/dot_general | solution.py:357
  10.6 0.6 pad_maximum_fusion.att_ref
  11.2 0.0 copy-done
  11.2 0.1 reshape.160
  11.4 0.7 reshape.161.owned_ref
  12.1 0.0 copy-done.1
  12.1 0.6 tile.11
  12.7 0.6 copy.30
  13.3 98.3 %layer.1 = bf16[16,2048]{1,0:T(8,128)(2,1)} custom-call(bf16[16,2048]{1,0:T(8,128)(2,1)} %pad_maximum_fusion.att_ref, s32[1,512]{1,0:T(1,128)} %bitcast.90, s32[2,256]{1,0:T(2,128)} %reshape.161.owned_ref, bf16[512,256]{1,0:T(8,128)(2,1)} %bitcast.85, bf16[2048,256]{1,0:T(8,128)(2,1)} %wo_ref.1, f32[8,128]{1,0:T(8,128)} %bitcast.89, ...), custom_call_target="tpu_custom_call" | custom-call | tf_op jit(solution)/shard_map/layer/pallas_call | solution.py:408
  111.6 1.5 %copy.48 = bf16[2,8,2048]{2,1,0:T(8,128)(2,1)} copy(bf16[2,8,2048]{2,1,0:T(8,128)(2,1)} %bitcast.84) | data formatting | bytes 131072
  (3 shorter events, 0.1 us)
Async XLA Ops:
  0.0 11.2 %copy-start = (s32[2,256]{1,0:T(2,128)S(1)}, s32[2,256]{1,0:T(2,128)}, u32[]{:S(2)}) copy-start(s32[2,256]{1,0:T(2,128)} %param.12) | copy-start | bytes 6148
  0.0 12.1 %copy-start.1 = (f32[256]{0:T(256)S(1)}, f32[256]{0:T(256)}, u32[]{:S(2)}) copy-start(f32[256]{0:T(256)} %param.15) | copy-start | bytes 3076

commit v2 on v0

v2 whole, which is shorter than its diff:
```python
import math

import jax
import jax.numpy as jnp
from jax import lax
from jax.experimental import pallas as pl
from jax.experimental.pallas import tpu as pltpu
from jax.sharding import PartitionSpec as P

MESH = pl.DeviceIdType.MESH
F32 = jnp.float32
BF16 = jnp.bfloat16
EPS = 1e-05
N = 4
MICRO = 2
COLS = (384, 384, 256)
STARTS = (0, 384, 768)
GATHER_PARTS = ((0, 16, 0, 384), (16, 16, 0, 384), (0, 32, 384, 128))
ORDERS = ((0, 1, 2), (1, 2, 0), (2, 0, 1))
W_CHUNKS = 8
W_SLOTS = 3


def dot(a, b):
    return jnp.dot(a, b, preferred_element_type=F32)


def layer_kernel(
    len_ref, query_ref, cache_ref, rows_ref, resid_ref, wo_ref, gain_ref, wg_ref, wd_ref,
    out_ref,
    kv, att_all, wo_all, resid_all, gain_all, w_raw, w_all, wd_all,
    proj_send, proj_recv, gathered, stats, acc, hid, pick,
    sums0, sums1, sums2, in10, in11, in12, t10, t11, t12,
    in20, in21, in22, t20, t21, t22, in30, in31, in32,
    res_own, res_send, res_recv,
    local_sem, sib_send, sib_recv, a_send, a_recv, b_send, b_recv,
    g_send, g_recv, s_send, s_recv, r_send, r_recv,
):
    g = lax.axis_index("grp")
    side = lax.axis_index("side")
    tp = lax.axis_index("tp")
    core = lax.rem(g, 2)
    y = lax.rem(g // 2, N)
    x = g // 8
    z = tp * 2 + side
    here = (x, y, z)
    xy = x * N + y
    shard = side * 2 + tp

    def device(cx, cy, cz, cc):
        return {"side": lax.rem(cz, 2), "grp": (cx * N + cy) * 2 + cc, "tp": cz // 2}

    def along(axis, k):
        moved = list(here)
        moved[axis] = lax.rem(here[axis] + k, N)
        return moved[axis], device(moved[0], moved[1], moved[2], core)

    sibling = device(x, y, z, 1 - core)
    all_sends = []

    def remote(src, dst, send, recv, target):
        copy = pltpu.make_async_remote_copy(
            src_ref=src, dst_ref=dst, send_sem=send, recv_sem=recv,
            device_id=target, device_id_type=MESH,
        )
        copy.start()
        all_sends.append(copy)
        return copy

    def local(src, dst, sem):
        copy = pltpu.make_async_copy(src, dst, sem)
        copy.start()
        return copy

    def received(copies):
        for copy in copies:
            copy.wait_recv()

    barrier = pltpu.get_barrier_semaphore()
    for axis in range(3):
        for k in (1, 2, 3):
            pl.semaphore_signal(barrier, inc=1, device_id=along(axis, k)[1], device_id_type=MESH)
    pl.semaphore_signal(barrier, inc=1, device_id=sibling, device_id_type=MESH)

    kv_loads = [
        [local(cache_ref.at[m, :, i], kv.at[m, i], local_sem.at[m * 2 + i]) for i in range(2)]
        for m in range(MICRO)
    ]
    raw_rows = w_raw.shape[1]

    def load_raw(chunk):
        return local(
            wg_ref.at[pl.ds(chunk * raw_rows, raw_rows)], w_raw.at[chunk % W_SLOTS], local_sem.at[8 + chunk]
        )

    raw_loads = {chunk: load_raw(chunk) for chunk in range(W_SLOTS)}
    wo_load = local(wo_ref, wo_all.at[core], local_sem.at[4])
    resid_load = local(resid_ref, resid_all.at[core], local_sem.at[5])
    wd_load = local(wd_ref, wd_all.at[core], local_sem.at[6])

    def attend(m):
        queries = query_ref[m].astype(F32)
        heads = queries.shape[1] // 128
        stacked = jnp.concatenate([queries[:, h * 128:(h + 1) * 128] for h in range(heads)], axis=0).astype(BF16)
        slot_id = lax.broadcasted_iota(jnp.int32, (heads * 8, 1), 0) % 8
        live = jnp.zeros((heads * 8, 1), jnp.int32)
        for s in range(8):
            live = jnp.where(slot_id == s, len_ref[m, s], live)
        kv_loads[m][0].wait()
        scores = None
        for s in range(8):
            one = lax.dot_general(stacked, kv[m, 0, s], (((1,), (1,)), ((), ())), preferred_element_type=F32)
            scores = one if s == 0 else jnp.where(slot_id == s, one, scores)
        position = lax.broadcasted_iota(jnp.int32, scores.shape, 1)
        scores = jnp.where(position < live, scores * (1.0 / math.sqrt(128)), -jnp.inf)
        top = jnp.max(scores, axis=1, keepdims=True)
        raised = jnp.exp(scores - top)
        total = jnp.sum(raised, axis=1, keepdims=True)
        weights = (raised / total).astype(BF16)
        kv_loads[m][1].wait()
        mixed = None
        for s in range(8):
            one = dot(weights, kv[m, 1, s])
            mixed = one if s == 0 else jnp.where(slot_id == s, one, mixed)
        halves = []
        for half in range(2):
            tiles = [mixed[(half * 8 + h) * 8:(half * 8 + h) * 8 + 8] for h in range(8)]
            halves.append(jnp.concatenate(tiles, axis=1))
        att_all[m, x, y] = jnp.concatenate(halves, axis=0).astype(BF16)

    def attended_phase(m, phase):
        copies = []
        for part in range(2):
            cols = pl.ds(part * 512, 512)
            axis = part if phase == 0 else 1 - part
            index = [x, y]
            if phase == 1:
                index[part] = slice(None)
            ref = att_all.at[m, index[0], index[1], :, cols]
            for k in (1, 2, 3):
                copies.append(remote(
                    ref, ref, a_send.at[m, phase, part, k - 1], a_recv.at[m, phase, part, k - 1], along(axis, k)[1]
                ))
        return copies

    p_out = lax.broadcasted_iota(jnp.int32, (256, 256), 0)
    p_in = lax.broadcasted_iota(jnp.int32, (256, 256), 1)
    order = jnp.where(p_in == (p_out % 64) * 4 + p_out // 64, 1.0, 0.0).astype(BF16)
    weight_copies = {}

    def untangle(chunk):
        raw_loads[chunk].wait()
        span = raw_rows // 512
        slot = chunk % W_SLOTS

        def step(u, _):
            row = pl.multiple_of(u * 512, 512)
            both = jnp.concatenate([w_raw[slot, pl.ds(row, 256)], w_raw[slot, pl.ds(row + 256, 256)]], axis=1)
            apart = dot(order, both).astype(BF16)
            base = pl.multiple_of((chunk * span + u) * 128, 128)
            for l in range(2):
                for c in range(2):
                    rows = slice((l * 2 + c) * 64, (l * 2 + c) * 64 + 64)
                    lanes = pl.ds(c * 256 + l * 128, 128)
                    w_all[core, pl.ds(base, 64), lanes] = apart[rows, 0:128]
                    w_all[core, pl.ds(base + 64, 64), lanes] = apart[rows, 128:256]
            return 0

        lax.fori_loop(0, span, step, 0)
        if chunk + W_SLOTS < W_CHUNKS:
            raw_loads[chunk + W_SLOTS] = load_raw(chunk + W_SLOTS)
        block = w_all.at[core, pl.ds(chunk * span * 128, span * 128)]
        weight_copies[chunk] = remote(block, block, sib_send.at[4 + chunk], sib_recv.at[4 + chunk], sibling)

    def slot_of(r, parity):
        return ((r // 8) * 2 + parity) * 8 + r % 8

    def choose(m):
        r = lax.broadcasted_iota(jnp.int32, (128, 256), 0)
        for i, parity in enumerate((core, 1 - core)):
            hit = jnp.where(slot_of(r, parity) == rows_ref[m:m + 1, :], 1.0, 0.0)
            turned = jnp.concatenate([jnp.transpose(hit[:, 0:128]), jnp.transpose(hit[:, 128:256])], axis=0)
            turned = turned.reshape(16, 2, 8, 128)
            even, odd = turned[:, 0].reshape(128, 128), turned[:, 1].reshape(128, 128)
            pick[m, i] = jnp.where(core == 0, even, odd)
            if i == 0:
                pick[m, 2] = jnp.where(core == 0, odd, even)

    def project(m):
        blocks = att_all[m].astype(F32).reshape(16, 2, 8, 1024)
        rows = jnp.concatenate([blocks[:, 0].reshape(128, 1024), blocks[:, 1].reshape(128, 1024)], axis=1).astype(BF16)
        for c in range(2):
            proj_send[m, :, :, c * 256:(c + 1) * 256] = dot(rows, wo_all[c]).astype(BF16).reshape(N, 32, 256)
        copies = []
        for k in (1, 2, 3):
            there, target = along(2, k)
            copies.append(remote(
                proj_send.at[m, there], proj_recv.at[m, k - 1], b_send.at[m, k - 1], b_recv.at[m, k - 1], target
            ))
        return copies

    def residual_rows(m):
        r = z * 32 + lax.broadcasted_iota(jnp.int32, (32, 256), 0)
        served = jnp.where(slot_of(r, core) == rows_ref[m:m + 1, :], 1.0, 0.0).astype(BF16)
        return jnp.concatenate([dot(served, resid_all[c, m * 256:(m + 1) * 256]) for c in range(2)], axis=1)

    def mix(m, resid_rows, gain_row):
        mixed = resid_rows + (
            (proj_send[m, z].astype(F32) + proj_recv[m, 0].astype(F32))
            + (proj_recv[m, 1].astype(F32) + proj_recv[m, 2].astype(F32))
        )
        gathered[m, x, y, z] = (mixed * gain_row).astype(BF16)
        squares = jnp.sum(mixed * mixed, axis=1, keepdims=True)
        tall = jnp.concatenate([jnp.broadcast_to(squares, (32, 128)), jnp.zeros((96, 128), F32)], axis=0)
        stats[m, x, y, z, 0:4] = jnp.transpose(tall)[0:4]
        stats[m, x, y, z, 4:6] = gain_all[0, 0:2]
        stats[m, x, y, z, 6:8] = gain_all[1, 0:2]

    def gather_phase(m, phase):
        copies = []
        for part, (row, rows, col, cols) in enumerate(GATHER_PARTS):
            axes = ORDERS[part]
            index = list(here)
            for done in axes[:phase]:
                index[done] = slice(None)
            block = gathered.at[m, index[0], index[1], index[2], pl.ds(row, rows), pl.ds(col, cols)]
            for k in (1, 2, 3):
                target = along(axes[phase], k)[1]
                copies.append(remote(
                    block, block, g_send.at[m, phase, part, k - 1], g_recv.at[m, phase, part, k - 1], target
                ))
                if part == 2:
                    tile = stats.at[m, index[0], index[1], index[2]]
                    copies.append(remote(
                        tile, tile, s_send.at[m, phase, k - 1], s_recv.at[m, phase, k - 1], target
                    ))
        return copies

    def feed(m):
        def multiply(i, _):
            block = jnp.concatenate([gathered[m, i, j].reshape(128, 512) for j in range(N)], axis=1)
            row = pl.multiple_of(i * 2048, 2048)
            for p in range(2):
                acc[:, p * 512:(p + 1) * 512] += dot(block, w_all[p, pl.ds(row, 2048), :])
            return 0

        acc[...] = jnp.zeros_like(acc)
        lax.fori_loop(0, N, multiply, 0)
        total = jnp.sum(stats[m].reshape(16, N, 8, 128), axis=0)
        columns = []
        for zz in range(N):
            spread = jnp.transpose(jnp.broadcast_to(total[zz, 0:1], (128, 128)))
            columns.append(spread[0:32])
        row_scale = lax.rsqrt(jnp.concatenate(columns, axis=0) * (1.0 / 8192) + EPS)
        row_scale = jnp.concatenate([row_scale, row_scale], axis=1)
        for p in range(2):
            gate = acc[:, p * 512:p * 512 + 256] * row_scale
            up = acc[:, p * 512 + 256:p * 512 + 512] * row_scale
            hid[m, core, :, p * 256:(p + 1) * 256] = (gate / (1.0 + jnp.exp(-gate)) * up).astype(BF16)
        block = hid.at[m, core]
        return remote(block, block, sib_send.at[12 + m], sib_recv.at[12 + m], sibling)

    def residual(m):
        row = pl.multiple_of(xy * 8, 8)
        wanted = jnp.concatenate([pick[m, 0, pl.ds(row, 8), :], pick[m, 2, pl.ds(row, 8), :]], axis=0).astype(BF16)
        found = [dot(wanted, gathered[m, shard, j].reshape(128, 512)) for j in range(N)]
        found = jnp.concatenate(found, axis=1)
        res_own[m] = found[0:8]
        res_send[m] = jnp.concatenate([found[8:16, 0:1024], found[8:16, 1024:2048]], axis=0).astype(BF16)
        return remote(res_send.at[m], res_recv.at[m], sib_send.at[14 + m], sib_recv.at[14 + m], sibling)

    sums = (sums0, sums1, sums2)
    in1 = (in10, in11, in12)
    t1 = (t10, t11, t12)
    in2 = (in20, in21, in22)
    t2 = (t20, t21, t22)
    in3 = (in30, in31, in32)

    def down(m):
        other = jnp.where(core == 0, hid[m, 1].astype(F32), hid[m, 0].astype(F32)).astype(BF16)
        ours = dot(pick[m, 0].astype(BF16), hid[m, core]) + dot(pick[m, 1].astype(BF16), other)
        ours = ours.astype(BF16)
        copies = [[], [], []]
        for part in range(3):
            width = COLS[part]
            for zz in range(N):
                base = ((zz % 2) * 2 + zz // 2) * 2048 + STARTS[part]
                halves = []
                for half in range(2):
                    lanes = pl.ds(base + half * 1024, width)
                    value = dot(ours[:, 0:256], wd_all[0, :, lanes]) + dot(ours[:, 256:512], wd_all[1, :, lanes])
                    halves.append(value.reshape(16, 1, 8, width))
                both = jnp.concatenate(halves, axis=1).reshape(N, N, 16, width)
                sums[part][m, :, :, zz] = both.astype(BF16)
            axis = ORDERS[part][0]
            for k in (1, 2, 3):
                there, target = along(axis, k)
                index = [slice(None)] * 3
                index[axis] = there
                copies[part].append(remote(
                    sums[part].at[m, index[0], index[1], index[2]], in1[part].at[m, k - 1],
                    r_send.at[m, 0, part, k - 1], r_recv.at[m, 0, part, k - 1], target,
                ))
        return copies

    def add(own, incoming):
        return (own.astype(F32) + incoming[0].astype(F32)) + (incoming[1].astype(F32) + incoming[2].astype(F32))

    def reduce_second(m, copies):
        started = [[], [], []]
        for part in range(3):
            received(copies[part])
            axes = ORDERS[part]
            for i in range(N):
                if axes[0] == 0:
                    own = sums[part][m, x, i]
                elif axes[0] == 1:
                    own = sums[part][m, i, y]
                else:
                    own = sums[part][m, i, :, z]
                t1[part][m, i] = add(own, [in1[part][m, q, i] for q in range(3)]).astype(BF16)
            first = axes[1] < axes[2]
            for k in (1, 2, 3):
                there, target = along(axes[1], k)
                src = t1[part].at[m, there] if first else t1[part].at[m, :, there]
                started[part].append(remote(
                    src, in2[part].at[m, k - 1],
                    r_send.at[m, 1, part, k - 1], r_recv.at[m, 1, part, k - 1], target,
                ))
        return started

    def reduce_third(m, copies):
        started = [[], [], []]
        for part in range(3):
            received(copies[part])
            axes = ORDERS[part]
            coord = here[axes[1]]
            own = t1[part][m, coord] if axes[1] < axes[2] else t1[part][m, :, coord]
            t2[part][m] = add(own, [in2[part][m, q] for q in range(3)]).astype(BF16)
            for k in (1, 2, 3):
                there, target = along(axes[2], k)
                started[part].append(remote(
                    t2[part].at[m, there], in3[part].at[m, k - 1],
                    r_send.at[m, 2, part, k - 1], r_recv.at[m, 2, part, k - 1], target,
                ))
        return started

    def finish(m, copies, res_copy):
        received([res_copy])
        pieces = [stats[m, shard, j, z, 4 + q:5 + q] for j in range(N) for q in range(4)]
        across = res_recv[m].astype(F32)
        across = jnp.concatenate([across[0:8], across[8:16]], axis=1)
        base = (res_own[m] + across) / jnp.concatenate(pieces, axis=1)
        for part in range(3):
            received(copies[part])
            own = t2[part][m, here[ORDERS[part][2]]]
            total = add(own, [in3[part][m, q] for q in range(3)])
            for half in range(2):
                start = half * 1024 + STARTS[part]
                lanes = slice(start, start + COLS[part])
                out_ref[m, :, lanes] = (base[:, lanes] + total[half * 8:half * 8 + 8]).astype(BF16)

    attend(0)
    gain_all[core, 0:2] = gain_ref[...]
    gain_all[core, 2:8] = jnp.zeros((6, 128), F32)
    pl.semaphore_wait(barrier, 10)
    a0 = attended_phase(0, 0)
    wo_copy = remote(wo_ref, wo_all.at[core], sib_send.at[0], sib_recv.at[0], sibling)
    resid_copy = remote(resid_ref, resid_all.at[core], sib_send.at[1], sib_recv.at[1], sibling)
    gain_copy = remote(gain_all.at[core], gain_all.at[core], sib_send.at[2], sib_recv.at[2], sibling)
    attend(1)
    received(a0)
    a0 = attended_phase(0, 1)
    a1 = attended_phase(1, 0)
    untangle(0)
    untangle(1)
    received(a1)
    a1 = attended_phase(1, 1)
    choose(0)
    choose(1)
    untangle(2)
    wo_load.wait()
    wo_copy.wait_recv()
    received(a0)
    b0 = project(0)
    wd_copy = remote(wd_ref, wd_all.at[core], sib_send.at[3], sib_recv.at[3], sibling)
    resid_load.wait()
    resid_copy.wait_recv()
    gain_copy.wait_recv()
    gain_row = jnp.concatenate(
        [gain_all[0, 0:1], gain_all[0, 1:2], gain_all[1, 0:1], gain_all[1, 1:2]], axis=1
    )
    resid0 = residual_rows(0)
    received(a1)
    b1 = project(1)
    resid1 = residual_rows(1)
    received(b0)
    mix(0, resid0, gain_row)
    g0 = gather_phase(0, 0)
    untangle(3)
    received(b1)
    mix(1, resid1, gain_row)
    g1 = gather_phase(1, 0)
    received(g0)
    g0 = gather_phase(0, 1)
    untangle(4)
    received(g1)
    g1 = gather_phase(1, 1)
    untangle(5)
    received(g0)
    g0 = gather_phase(0, 2)
    received(g1)
    g1 = gather_phase(1, 2)
    untangle(6)
    untangle(7)
    received(weight_copies.values())
    received(g0)
    h0 = feed(0)
    c0 = residual(0)
    wd_load.wait()
    wd_copy.wait_recv()
    received([h0])
    r0 = down(0)
    received(g1)
    h1 = feed(1)
    c1 = residual(1)
    r0 = reduce_second(0, r0)
    received([h1])
    r1 = down(1)
    r0 = reduce_third(0, r0)
    r1 = reduce_second(1, r1)
    finish(0, r0, c0)
    r1 = reduce_third(1, r1)
    finish(1, r1, c1)

    for copy in all_sends:
        copy.wait_send()


def shards(query, cache, cache_len, row_slot, resid, w_out, norm_gain, w_gate_up, w_down):
    raw = w_gate_up.reshape(8192, 2, 2, 128).transpose(0, 2, 1, 3).reshape(32768, 128)
    vmem = pl.BlockSpec(memory_space=pltpu.VMEM)
    smem = pl.BlockSpec(memory_space=pltpu.SMEM)
    hbm = pl.BlockSpec(memory_space=pl.ANY)
    sem = pltpu.SemaphoreType.DMA
    scratch = [
        pltpu.VMEM((MICRO, 2, 8, 1024, 128), BF16),
        pltpu.VMEM((MICRO, N, N, 16, 1024), BF16),
        pltpu.VMEM((2, 2048, 256), BF16),
        pltpu.VMEM((2, 512, 256), BF16),
        pltpu.VMEM((2, 8, 128), F32),
        pltpu.VMEM((W_SLOTS, 32768 // W_CHUNKS, 128), BF16),
        pltpu.VMEM((2, 8192, 512), BF16),
        pltpu.VMEM((2, 256, 8192), BF16),
        pltpu.VMEM((MICRO, N, 32, 512), BF16),
        pltpu.VMEM((MICRO, 3, 32, 512), BF16),
        pltpu.VMEM((MICRO, N, N, N, 32, 512), BF16),
        pltpu.VMEM((MICRO, N, N, N, 8, 128), F32),
        pltpu.VMEM((128, 1024), F32),
        pltpu.VMEM((MICRO, 2, 128, 512), BF16),
        pltpu.VMEM((MICRO, 3, 128, 128), F32),
    ]
    scratch += [pltpu.VMEM((MICRO, N, N, N, 16, c), BF16) for c in COLS]
    scratch += [pltpu.VMEM((MICRO, 3, N, N, 16, c), BF16) for c in COLS]
    scratch += [pltpu.VMEM((MICRO, N, N, 16, c), BF16) for c in COLS]
    scratch += [pltpu.VMEM((MICRO, 3, N, 16, c), BF16) for c in COLS]
    scratch += [pltpu.VMEM((MICRO, N, 16, c), BF16) for c in COLS]
    scratch += [pltpu.VMEM((MICRO, 3, 16, c), BF16) for c in COLS]
    scratch += [
        pltpu.VMEM((MICRO, 8, 2048), F32),
        pltpu.VMEM((MICRO, 16, 1024), BF16),
        pltpu.VMEM((MICRO, 16, 1024), BF16),
    ]
    scratch += [
        sem((8 + W_CHUNKS,)),
        sem((16,)), sem((16,)),
        sem((MICRO, 2, 2, 3)), sem((MICRO, 2, 2, 3)),
        sem((MICRO, 3)), sem((MICRO, 3)),
        sem((MICRO, 3, 3, 3)), sem((MICRO, 3, 3, 3)),
        sem((MICRO, 3, 3)), sem((MICRO, 3, 3)),
        sem((MICRO, 3, 3, 3)), sem((MICRO, 3, 3, 3)),
    ]
    return pl.pallas_call(
        layer_kernel,
        out_shape=jax.ShapeDtypeStruct((MICRO, 8, 2048), BF16),
        in_specs=[smem, vmem, hbm, vmem, hbm, hbm, vmem, hbm, hbm],
        out_specs=vmem,
        scratch_shapes=scratch,
        compiler_params=pltpu.CompilerParams(
            collective_id=0, has_side_effects=True, vmem_limit_bytes=62 * 1024 * 1024
        ),
        name="layer",
    )(
        cache_len, query, cache.reshape(MICRO, 8, 2, 1024, 128), row_slot, resid.reshape(512, 256), w_out,
        norm_gain.reshape(2, 128), raw, w_down,
    )


def solution(mesh):
    placed = (
        P(None, "grp", ("side", "tp")),
        P(None, "grp", None, ("side", "tp"), None, None),
        P(None, "grp"),
        P(),
        P(None, None, "grp"),
        P(("side", "tp"), "grp"),
        P("grp"),
        P(None, None, ("side", "grp", "tp")),
        P(("side", "grp", "tp"), None),
    )
    return jax.shard_map(
        shards,
        mesh=mesh,
        in_specs=placed,
        out_specs=P(None, "grp", ("side", "tp")),
        check_vma=False,
    )
```

time: 571 us -> 90.2 us (0.16)
  waiting for transfers between devices: 422 us -> 0 us
  Pallas kernels: 0 us -> 88.5 us
  blocking collectives: 65 us -> 0 us
  matrix products: 35.7 us -> 0 us
  local copies, waits for them, and re-layouts: 24.7 us -> 1.47 us
  between operations: 13.4 us -> 0.01 us
  other arithmetic: 9.09 us -> 0 us
    reduce_scatter x4 -> x0, waiting for transfers between devices: 234 us -> none  [the longest x2 188 us: shards(): lax.psum_scatter(lax.dynamic_update_slice_in_dim(partial_value, current +...]
    all_gather x4 -> x0, waiting for transfers between devices: 144 us -> none  [the longest x2 80.7 us: shards(): lax.all_gather(attended, 'grp', axis=0, tiled=True)]
    pallas_call x0 -> x1, Pallas kernels: none -> 88.5 us  [shards(): pl.pallas_call(layer_kernel, out_shape=jax.ShapeDtypeStruct((MICRO, 8, 20...]
    psum x1 -> x0, blocking collectives: 65 us -> none  [shards(): squares = lax.psum(jnp.sum(mixed * mixed, axis=1), 'grp')]
    psum x1 -> x0, waiting for transfers between devices: 42.8 us -> none  [shards(): mixed = residual_rows + lax.psum(projected, ('side', 'tp'))]
    dot_general x8 -> x0, matrix products: 30.8 us -> none  [the longest x2 14.3 us: shards(): jnp.dot(lax.all_gather(normed, 'grp', axis=1, tiled=True), gate_flat, pre...]
    dot_general x1 -> x0, local copies, waits for them, and re-layouts: 11.8 us -> none  [shards(): jnp.dot(lax.all_gather(normed, 'grp', axis=1, tiled=True), gate_flat, pre...]
    unnamed x22 -> x1, local copies, waits for them, and re-layouts: 10.1 us -> 1.47 us
  transfers between devices with their start and end apart: 9 -> 0, of which waited for: 9 -> 0; matrix products, arithmetic and copies ran while one was open for 7% -> 0% of each run, Pallas kernels for 0% -> 0%
where the time goes in v2:
time: 90.2 us; the launch traced here: 90 us
  Pallas kernels  88.5 us (98%)
  local copies, waits for them, and re-layouts  1.47 us (2%)
    pallas_call x1, Pallas kernels, shards(): pl.pallas_call(layer_kernel, out_shape=jax.ShapeDtypeStruct((MICRO, 8, 20...  88.5 us

profile of v2, /device:TPU:0, one launch (start us, length us, event | category | flops | bytes accessed | tf_op | source)
XLA Modules:
  0.0 90.0 jit_solution(5007095617937604443)
XLA Ops:
  0.0 88.5 %layer.1 = bf16[2,8,2048]{2,1,0:T(8,128)(2,1)} custom-call(s32[2,8]{1,0:T(2,128)} %len_ref.1, bf16[2,8,2048]{2,1,0:T(8,128)(2,1)} %query_ref.1, bf16[2,8,2,1024,128]{4,3,2,1,0:T(8,128)(2,1)} %bitcast.8, s32[2,256]{1,0:T(2,128)} %rows_ref.1, bf16[512,256]{1,0:T(8,128)(2,1)} %bitcast.10, bf16[2048,256]{1,0:T(8,128)(2,1)} %wo_ref.1, f32[2,128]{1,0:T(2,128)} %bitcast.11, ...), custom_call_target="tpu_custom_call" | custom-call | tf_op jit(solution)/shard_map/layer/pallas_call | solution.py:483
  88.5 1.5 %copy.12 = bf16[2,8,2048]{2,1,0:T(8,128)(2,1)} copy(bf16[2,8,2048]{2,1,0:T(8,128)(2,1)} %layer.1) | data formatting | bytes 131072

commit v3 on v2

--- a/solution.py
+++ b/solution.py
@@ -29,8 +29,8 @@
     len_ref, query_ref, cache_ref, rows_ref, resid_ref, wo_ref, gain_ref, wg_ref, wd_ref,
     out_ref,
     kv, att_all, wo_all, resid_all, gain_all, w_raw, w_all, wd_all,
-    proj_send, proj_recv, gathered, stats, acc, hid, pick,
-    sums0, sums1, sums2, in10, in11, in12, t10, t11, t12,
+    proj_send, proj_recv, gathered, stats, hid, pick,
+    sums0, sums1, sums2, via0, via1, via2, in10, in11, in12, t10, t11, t12,
     in20, in21, in22, t20, t21, t22, in30, in31, in32,
     res_own, res_send, res_recv,
     local_sem, sib_send, sib_recv, a_send, a_recv, b_send, b_recv,
@@ -82,10 +82,10 @@
             pl.semaphore_signal(barrier, inc=1, device_id=along(axis, k)[1], device_id_type=MESH)
     pl.semaphore_signal(barrier, inc=1, device_id=sibling, device_id_type=MESH)
 
-    kv_loads = [
-        [local(cache_ref.at[m, :, i], kv.at[m, i], local_sem.at[m * 2 + i]) for i in range(2)]
-        for m in range(MICRO)
-    ]
+    def load_kv(m):
+        return [local(cache_ref.at[m, :, i], kv.at[m, i], local_sem.at[m * 2 + i]) for i in range(2)]
+
+    kv_loads = {0: load_kv(0), 1: load_kv(1)}
     raw_rows = w_raw.shape[1]
 
     def load_raw(chunk):
@@ -93,10 +93,14 @@
             wg_ref.at[pl.ds(chunk * raw_rows, raw_rows)], w_raw.at[chunk % W_SLOTS], local_sem.at[8 + chunk]
         )
 
-    raw_loads = {chunk: load_raw(chunk) for chunk in range(W_SLOTS)}
-    wo_load = local(wo_ref, wo_all.at[core], local_sem.at[4])
-    resid_load = local(resid_ref, resid_all.at[core], local_sem.at[5])
-    wd_load = local(wd_ref, wd_all.at[core], local_sem.at[6])
+    raw_loads = {}
+    other_loads = {}
+
+    def load_rest():
+        other_loads["wo"] = local(wo_ref, wo_all.at[core], local_sem.at[4])
+        other_loads["resid"] = local(resid_ref, resid_all.at[core], local_sem.at[5])
+        for chunk in range(W_SLOTS):
+            raw_loads[chunk] = load_raw(chunk)
 
     def attend(m):
         queries = query_ref[m].astype(F32)
@@ -107,6 +111,8 @@
         for s in range(8):
             live = jnp.where(slot_id == s, len_ref[m, s], live)
         kv_loads[m][0].wait()
+        if m == 0:
+            load_rest()
         scores = None
         for s in range(8):
             one = lax.dot_general(stacked, kv[m, 0, s], (((1,), (1,)), ((), ())), preferred_element_type=F32)
@@ -153,20 +159,16 @@
         span = raw_rows // 512
         slot = chunk % W_SLOTS
 
-        def step(u, _):
-            row = pl.multiple_of(u * 512, 512)
-            both = jnp.concatenate([w_raw[slot, pl.ds(row, 256)], w_raw[slot, pl.ds(row + 256, 256)]], axis=1)
-            apart = dot(order, both).astype(BF16)
-            base = pl.multiple_of((chunk * span + u) * 128, 128)
-            for l in range(2):
-                for c in range(2):
-                    rows = slice((l * 2 + c) * 64, (l * 2 + c) * 64 + 64)
-                    lanes = pl.ds(c * 256 + l * 128, 128)
-                    w_all[core, pl.ds(base, 64), lanes] = apart[rows, 0:128]
-                    w_all[core, pl.ds(base + 64, 64), lanes] = apart[rows, 128:256]
-            return 0
-
-        lax.fori_loop(0, span, step, 0)
+        tiles = raw_rows // 256
+        mixed = jnp.concatenate([w_raw[slot, q * 256:(q + 1) * 256] for q in range(tiles)], axis=1)
+        apart = dot(order, mixed)
+        for l in range(2):
+            for c in range(2):
+                rows = slice((l * 2 + c) * 64, (l * 2 + c) * 64 + 64)
+                lanes = pl.ds(c * 256 + l * 128, 128)
+                for q in range(tiles):
+                    base = (chunk * tiles + q) * 64
+                    w_all[core, pl.ds(base, 64), lanes] = apart[rows, q * 128:(q + 1) * 128].astype(BF16)
         if chunk + W_SLOTS < W_CHUNKS:
             raw_loads[chunk + W_SLOTS] = load_raw(chunk + W_SLOTS)
         block = w_all.at[core, pl.ds(chunk * span * 128, span * 128)]
@@ -236,16 +238,43 @@
                     ))
         return copies
 
+    def gather_block(m, part, coord, half):
+        axis = ORDERS[part][2]
+        row, rows, col, cols = GATHER_PARTS[part]
+        index = [slice(None)] * 3
+        index[min(ORDERS[part][:2])] = pl.ds(half * 2, 2)
+        index[axis] = coord
+        return gathered.at[m, index[0], index[1], index[2], pl.ds(row, rows), pl.ds(col, cols)]
+
+    def gather_step(m, part, coord, half, k, slot):
+        block = gather_block(m, part, coord, half)
+        return remote(
+            block, block, g_send.at[m, 2, part, slot], g_recv.at[m, 2, part, slot], along(ORDERS[part][2], k)[1]
+        )
+
+    def gather_last(m):
+        own = [here[ORDERS[part][2]] for part in range(3)]
+        early = [
+            (gather_step(m, part, own[part], 0, 1, 0), gather_step(m, part, own[part], 1, 3, 1)) for part in range(3)
+        ]
+        late = []
+        for part in range(3):
+            late.append(gather_step(m, part, own[part], 1, 1, 2))
+            late.append(gather_step(m, part, own[part], 0, 3, 3))
+        for k in (1, 2, 3):
+            tile = stats.at[m, :, y]
+            late.append(remote(tile, tile, s_send.at[m, 2, k - 1], s_recv.at[m, 2, k - 1], along(1, k)[1]))
+        return early, late
+
+    def gather_pass(m, early, late):
+        for part in range(3):
+            axis = ORDERS[part][2]
+            early[part][0].wait_recv()
+            late.append(gather_step(m, part, along(axis, 3)[0], 0, 1, 4))
+            early[part][1].wait_recv()
+            late.append(gather_step(m, part, along(axis, 1)[0], 1, 3, 5))
+
     def feed(m):
-        def multiply(i, _):
-            block = jnp.concatenate([gathered[m, i, j].reshape(128, 512) for j in range(N)], axis=1)
-            row = pl.multiple_of(i * 2048, 2048)
-            for p in range(2):
-                acc[:, p * 512:(p + 1) * 512] += dot(block, w_all[p, pl.ds(row, 2048), :])
-            return 0
-
-        acc[...] = jnp.zeros_like(acc)
-        lax.fori_loop(0, N, multiply, 0)
         total = jnp.sum(stats[m].reshape(16, N, 8, 128), axis=0)
         columns = []
         for zz in range(N):
@@ -253,9 +282,12 @@
             columns.append(spread[0:32])
         row_scale = lax.rsqrt(jnp.concatenate(columns, axis=0) * (1.0 / 8192) + EPS)
         row_scale = jnp.concatenate([row_scale, row_scale], axis=1)
+        features = jnp.concatenate(
+            [gathered[m, i, j].reshape(128, 512) for i in range(N) for j in range(N)], axis=1
+        )
         for p in range(2):
-            gate = acc[:, p * 512:p * 512 + 256] * row_scale
-            up = acc[:, p * 512 + 256:p * 512 + 512] * row_scale
+            gate = dot(features, w_all[p, :, 0:256]) * row_scale
+            up = dot(features, w_all[p, :, 256:512]) * row_scale
             hid[m, core, :, p * 256:(p + 1) * 256] = (gate / (1.0 + jnp.exp(-gate)) * up).astype(BF16)
         block = hid.at[m, core]
         return remote(block, block, sib_send.at[12 + m], sib_recv.at[12 + m], sibling)
@@ -270,11 +302,26 @@
         return remote(res_send.at[m], res_recv.at[m], sib_send.at[14 + m], sib_recv.at[14 + m], sibling)
 
     sums = (sums0, sums1, sums2)
+    via = (via0, via1, via2)
     in1 = (in10, in11, in12)
     t1 = (t10, t11, t12)
     in2 = (in20, in21, in22)
     t2 = (t20, t21, t22)
     in3 = (in30, in31, in32)
+
+    def sum_index(part, coord, half):
+        axis = ORDERS[part][0]
+        index = [slice(None)] * 3
+        index[1 if axis == 0 else 0] = pl.ds(half * 2, 2)
+        index[axis] = coord
+        return index
+
+    def reduce_step(m, part, coord, half, dst, k, slot):
+        index = sum_index(part, coord, half)
+        return remote(
+            sums[part].at[m, index[0], index[1], index[2]], dst,
+            r_send.at[m, 0, part, slot], r_recv.at[m, 0, part, slot], along(ORDERS[part][0], k)[1],
+        )
 
     def down(m):
         other = jnp.where(core == 0, hid[m, 1].astype(F32), hid[m, 0].astype(F32)).astype(BF16)
@@ -292,24 +339,38 @@
                     halves.append(value.reshape(16, 1, 8, width))
                 both = jnp.concatenate(halves, axis=1).reshape(N, N, 16, width)
                 sums[part][m, :, :, zz] = both.astype(BF16)
-            axis = ORDERS[part][0]
-            for k in (1, 2, 3):
-                there, target = along(axis, k)
-                index = [slice(None)] * 3
-                index[axis] = there
-                copies[part].append(remote(
-                    sums[part].at[m, index[0], index[1], index[2]], in1[part].at[m, k - 1],
-                    r_send.at[m, 0, part, k - 1], r_recv.at[m, 0, part, k - 1], target,
+            far = along(ORDERS[part][0], 2)[0]
+            ahead, back = along(ORDERS[part][0], 1)[0], along(ORDERS[part][0], 3)[0]
+            copies[part] = [
+                reduce_step(m, part, far, 0, via[part].at[m, 0], 1, 0),
+                reduce_step(m, part, far, 1, via[part].at[m, 1], 3, 1),
+                reduce_step(m, part, ahead, 1, in1[part].at[m, 0, pl.ds(2, 2)], 1, 2),
+                reduce_step(m, part, back, 0, in1[part].at[m, 1, pl.ds(0, 2)], 3, 3),
+            ]
+        return copies
+
+    def reduce_pass(m, copies):
+        for part in range(3):
+            for half, k in ((0, 1), (1, 3)):
+                there = along(ORDERS[part][0], k)[0]
+                copies[part][half].wait_recv()
+                index = sum_index(part, there, half)
+                own = sums[part][m, index[0], index[1], index[2]].astype(F32)
+                sums[part][m, index[0], index[1], index[2]] = (own + via[part][m, half].astype(F32)).astype(BF16)
+                copies[part].append(reduce_step(
+                    m, part, there, half, in1[part].at[m, half, pl.ds(half * 2, 2)], k, 4 + half
                 ))
-        return copies
 
     def add(own, incoming):
-        return (own.astype(F32) + incoming[0].astype(F32)) + (incoming[1].astype(F32) + incoming[2].astype(F32))
+        total = own.astype(F32)
+        for term in incoming:
+            total = total + term.astype(F32)
+        return total
 
     def reduce_second(m, copies):
         started = [[], [], []]
         for part in range(3):
-            received(copies[part])
+            received(copies[part][2:])
             axes = ORDERS[part]
             for i in range(N):
                 if axes[0] == 0:
@@ -318,7 +379,7 @@
                     own = sums[part][m, i, y]
                 else:
                     own = sums[part][m, i, :, z]
-                t1[part][m, i] = add(own, [in1[part][m, q, i] for q in range(3)]).astype(BF16)
+                t1[part][m, i] = add(own, [in1[part][m, q, i] for q in range(2)]).astype(BF16)
             first = axes[1] < axes[2]
             for k in (1, 2, 3):
                 there, target = along(axes[1], k)
@@ -369,64 +430,69 @@
     resid_copy = remote(resid_ref, resid_all.at[core], sib_send.at[1], sib_recv.at[1], sibling)
     gain_copy = remote(gain_all.at[core], gain_all.at[core], sib_send.at[2], sib_recv.at[2], sibling)
     attend(1)
+    a1 = attended_phase(1, 0)
     received(a0)
     a0 = attended_phase(0, 1)
-    a1 = attended_phase(1, 0)
+    wd_load = local(wd_ref, wd_all.at[core], local_sem.at[6])
+    wd_copy = remote(wd_ref, wd_all.at[core], sib_send.at[3], sib_recv.at[3], sibling)
     untangle(0)
     untangle(1)
+    untangle(2)
     received(a1)
     a1 = attended_phase(1, 1)
     choose(0)
     choose(1)
-    untangle(2)
-    wo_load.wait()
+    untangle(3)
+    other_loads["wo"].wait()
     wo_copy.wait_recv()
     received(a0)
     b0 = project(0)
-    wd_copy = remote(wd_ref, wd_all.at[core], sib_send.at[3], sib_recv.at[3], sibling)
-    resid_load.wait()
+    other_loads["resid"].wait()
     resid_copy.wait_recv()
     gain_copy.wait_recv()
     gain_row = jnp.concatenate(
         [gain_all[0, 0:1], gain_all[0, 1:2], gain_all[1, 0:1], gain_all[1, 1:2]], axis=1
     )
     resid0 = residual_rows(0)
+    untangle(4)
     received(a1)
     b1 = project(1)
     resid1 = residual_rows(1)
+    untangle(5)
     received(b0)
     mix(0, resid0, gain_row)
     g0 = gather_phase(0, 0)
-    untangle(3)
     received(b1)
     mix(1, resid1, gain_row)
     g1 = gather_phase(1, 0)
+    untangle(6)
     received(g0)
     g0 = gather_phase(0, 1)
-    untangle(4)
     received(g1)
     g1 = gather_phase(1, 1)
-    untangle(5)
+    untangle(7)
     received(g0)
-    g0 = gather_phase(0, 2)
+    g0, l0 = gather_last(0)
     received(g1)
-    g1 = gather_phase(1, 2)
-    untangle(6)
-    untangle(7)
+    gather_pass(0, g0, l0)
+    g1, l1 = gather_last(1)
+    gather_pass(1, g1, l1)
     received(weight_copies.values())
-    received(g0)
+    received(l0)
     h0 = feed(0)
     c0 = residual(0)
     wd_load.wait()
     wd_copy.wait_recv()
     received([h0])
     r0 = down(0)
-    received(g1)
+    received(l1)
     h1 = feed(1)
     c1 = residual(1)
-    r0 = reduce_second(0, r0)
+    reduce_pass(0, r0)
     received([h1])
     r1 = down(1)
+    r0 = reduce_second(0, r0)
+    reduce_pass(1, r1)
     r0 = reduce_third(0, r0)
     r1 = reduce_second(1, r1)
     finish(0, r0, c0)
@@ -456,12 +522,12 @@
         pltpu.VMEM((MICRO, 3, 32, 512), BF16),
         pltpu.VMEM((MICRO, N, N, N, 32, 512), BF16),
         pltpu.VMEM((MICRO, N, N, N, 8, 128), F32),
-        pltpu.VMEM((128, 1024), F32),
         pltpu.VMEM((MICRO, 2, 128, 512), BF16),
         pltpu.VMEM((MICRO, 3, 128, 128), F32),
     ]
     scratch += [pltpu.VMEM((MICRO, N, N, N, 16, c), BF16) for c in COLS]
-    scratch += [pltpu.VMEM((MICRO, 3, N, N, 16, c), BF16) for c in COLS]
+    scratch += [pltpu.VMEM((MICRO, 2, 2, N, 16, c), BF16) for c in COLS]
+    scratch += [pltpu.VMEM((MICRO, 2, N, N, 16, c), BF16) for c in COLS]
     scratch += [pltpu.VMEM((MICRO, N, N, 16, c), BF16) for c in COLS]
     scratch += [pltpu.VMEM((MICRO, 3, N, 16, c), BF16) for c in COLS]
     scratch += [pltpu.VMEM((MICRO, N, 16, c), BF16) for c in COLS]
@@ -476,9 +542,9 @@
         sem((16,)), sem((16,)),
         sem((MICRO, 2, 2, 3)), sem((MICRO, 2, 2, 3)),
         sem((MICRO, 3)), sem((MICRO, 3)),
-        sem((MICRO, 3, 3, 3)), sem((MICRO, 3, 3, 3)),
+        sem((MICRO, 3, 3, 6)), sem((MICRO, 3, 3, 6)),
         sem((MICRO, 3, 3)), sem((MICRO, 3, 3)),
-        sem((MICRO, 3, 3, 3)), sem((MICRO, 3, 3, 3)),
+        sem((MICRO, 3, 3, 6)), sem((MICRO, 3, 3, 6)),
     ]
     return pl.pallas_call(
         layer_kernel,

time: 90.2 us -> 83.8 us (0.929)
  Pallas kernels: 88.5 us -> 82 us
    pallas_call x1, Pallas kernels: 88.5 us -> 82 us  [shards(): pl.pallas_call(layer_kernel, out_shape=jax.ShapeDtypeStruct((MICRO, 8, 20...]
where the time goes in v3:
time: 83.8 us; the launch traced here: 83.4 us
  Pallas kernels  82 us (98%)
  local copies, waits for them, and re-layouts  1.47 us (2%)
    pallas_call x1, Pallas kernels, shards(): pl.pallas_call(layer_kernel, out_shape=jax.ShapeDtypeStruct((MICRO, 8, 20...  82 us

profile of v3, /device:TPU:0, one launch (start us, length us, event | category | flops | bytes accessed | tf_op | source)
XLA Modules:
  0.0 83.4 jit_solution(5552132141849398781)
XLA Ops:
  0.0 82.0 %layer.1 = bf16[2,8,2048]{2,1,0:T(8,128)(2,1)} custom-call(s32[2,8]{1,0:T(2,128)} %len_ref.1, bf16[2,8,2048]{2,1,0:T(8,128)(2,1)} %query_ref.1, bf16[2,8,2,1024,128]{4,3,2,1,0:T(8,128)(2,1)} %bitcast.8, s32[2,256]{1,0:T(2,128)} %rows_ref.1, bf16[512,256]{1,0:T(8,128)(2,1)} %bitcast.10, bf16[2048,256]{1,0:T(8,128)(2,1)} %wo_ref.1, f32[2,128]{1,0:T(2,128)} %bitcast.11, ...), custom_call_target="tpu_custom_call" | custom-call | tf_op jit(solution)/shard_map/layer/pallas_call | solution.py:549
  82.0 1.5 %copy.12 = bf16[2,8,2048]{2,1,0:T(8,128)(2,1)} copy(bf16[2,8,2048]{2,1,0:T(8,128)(2,1)} %layer.1) | data formatting | bytes 131072

commit v4 on v3

--- a/solution.py
+++ b/solution.py
@@ -26,9 +26,9 @@
 
 
 def layer_kernel(
-    len_ref, query_ref, cache_ref, rows_ref, resid_ref, wo_ref, gain_ref, wg_ref, wd_ref,
+    len_ref, query_in, cache_ref, rows_in, resid_ref, wo_ref, gain_in, wg_ref, wd_ref,
     out_ref,
-    kv, att_all, wo_all, resid_all, gain_all, w_raw, w_all, wd_all,
+    query_ref, rows_ref, gain_ref, kv, att_all, wo_all, resid_all, gain_all, w_raw, w_all, wd_all,
     proj_send, proj_recv, gathered, stats, hid, pick,
     sums0, sums1, sums2, via0, via1, via2, in10, in11, in12, t10, t11, t12,
     in20, in21, in22, t20, t21, t22, in30, in31, in32,
@@ -72,9 +72,16 @@
         copy.start()
         return copy
 
+    def drain(count):
+        for copy in all_sends[:count]:
+            copy.wait_send()
+        del all_sends[:count]
+
     def received(copies):
         for copy in copies:
             copy.wait_recv()
+
+    query_load = local(query_in, query_ref, local_sem.at[8 + W_CHUNKS])
 
     barrier = pltpu.get_barrier_semaphore()
     for axis in range(3):
@@ -86,6 +93,8 @@
         return [local(cache_ref.at[m, :, i], kv.at[m, i], local_sem.at[m * 2 + i]) for i in range(2)]
 
     kv_loads = {0: load_kv(0), 1: load_kv(1)}
+    rows_load = local(rows_in, rows_ref, local_sem.at[7])
+    gain_load = local(gain_in, gain_ref, local_sem.at[9 + W_CHUNKS])
     raw_rows = w_raw.shape[1]
 
     def load_raw(chunk):
@@ -103,6 +112,8 @@
             raw_loads[chunk] = load_raw(chunk)
 
     def attend(m):
+        if m == 0:
+            query_load.wait()
         queries = query_ref[m].astype(F32)
         heads = queries.shape[1] // 128
         stacked = jnp.concatenate([queries[:, h * 128:(h + 1) * 128] for h in range(heads)], axis=0).astype(BF16)
@@ -156,7 +167,6 @@
 
     def untangle(chunk):
         raw_loads[chunk].wait()
-        span = raw_rows // 512
         slot = chunk % W_SLOTS
 
         tiles = raw_rows // 256
@@ -171,6 +181,9 @@
                     w_all[core, pl.ds(base, 64), lanes] = apart[rows, q * 128:(q + 1) * 128].astype(BF16)
         if chunk + W_SLOTS < W_CHUNKS:
             raw_loads[chunk + W_SLOTS] = load_raw(chunk + W_SLOTS)
+
+    def share(chunk):
+        span = raw_rows // 512
         block = w_all.at[core, pl.ds(chunk * span * 128, span * 128)]
         weight_copies[chunk] = remote(block, block, sib_send.at[4 + chunk], sib_recv.at[4 + chunk], sibling)
 
@@ -422,81 +435,97 @@
                 out_ref[m, :, lanes] = (base[:, lanes] + total[half * 8:half * 8 + 8]).astype(BF16)
 
     attend(0)
+    attend(1)
+    gain_load.wait()
     gain_all[core, 0:2] = gain_ref[...]
     gain_all[core, 2:8] = jnp.zeros((6, 128), F32)
     pl.semaphore_wait(barrier, 10)
     a0 = attended_phase(0, 0)
+    a1 = attended_phase(1, 0)
     wo_copy = remote(wo_ref, wo_all.at[core], sib_send.at[0], sib_recv.at[0], sibling)
     resid_copy = remote(resid_ref, resid_all.at[core], sib_send.at[1], sib_recv.at[1], sibling)
     gain_copy = remote(gain_all.at[core], gain_all.at[core], sib_send.at[2], sib_recv.at[2], sibling)
-    attend(1)
-    a1 = attended_phase(1, 0)
+    wd_load = local(wd_ref, wd_all.at[core], local_sem.at[6])
+    for chunk in range(0, 2):
+        untangle(chunk)
+        share(chunk)
     received(a0)
     a0 = attended_phase(0, 1)
-    wd_load = local(wd_ref, wd_all.at[core], local_sem.at[6])
-    wd_copy = remote(wd_ref, wd_all.at[core], sib_send.at[3], sib_recv.at[3], sibling)
-    untangle(0)
-    untangle(1)
-    untangle(2)
     received(a1)
     a1 = attended_phase(1, 1)
+    wd_copy = remote(wd_ref, wd_all.at[core], sib_send.at[3], sib_recv.at[3], sibling)
+    rows_load.wait()
     choose(0)
     choose(1)
-    untangle(3)
+    for chunk in range(2, 4):
+        untangle(chunk)
+        share(chunk)
     other_loads["wo"].wait()
     wo_copy.wait_recv()
-    received(a0)
-    b0 = project(0)
     other_loads["resid"].wait()
     resid_copy.wait_recv()
     gain_copy.wait_recv()
+    received(a0)
+    b0 = project(0)
     gain_row = jnp.concatenate(
         [gain_all[0, 0:1], gain_all[0, 1:2], gain_all[1, 0:1], gain_all[1, 1:2]], axis=1
     )
     resid0 = residual_rows(0)
+    resid1 = residual_rows(1)
     untangle(4)
+    share(4)
     received(a1)
     b1 = project(1)
-    resid1 = residual_rows(1)
     untangle(5)
+    share(5)
     received(b0)
     mix(0, resid0, gain_row)
     g0 = gather_phase(0, 0)
     received(b1)
     mix(1, resid1, gain_row)
     g1 = gather_phase(1, 0)
-    untangle(6)
+    for chunk in range(6, W_CHUNKS):
+        untangle(chunk)
+        share(chunk)
     received(g0)
     g0 = gather_phase(0, 1)
     received(g1)
     g1 = gather_phase(1, 1)
-    untangle(7)
     received(g0)
+    early = len(all_sends)
     g0, l0 = gather_last(0)
     received(g1)
     gather_pass(0, g0, l0)
     g1, l1 = gather_last(1)
     gather_pass(1, g1, l1)
+    drain(early)
+    early = len(all_sends)
     received(weight_copies.values())
     received(l0)
     h0 = feed(0)
-    c0 = residual(0)
     wd_load.wait()
     wd_copy.wait_recv()
     received([h0])
     r0 = down(0)
+    c0 = residual(0)
     received(l1)
     h1 = feed(1)
-    c1 = residual(1)
     reduce_pass(0, r0)
     received([h1])
+    middle = len(all_sends)
     r1 = down(1)
+    c1 = residual(1)
+    drain(early)
+    middle = middle - early
     r0 = reduce_second(0, r0)
     reduce_pass(1, r1)
     r0 = reduce_third(0, r0)
     r1 = reduce_second(1, r1)
+    drain(middle)
+    early = len(all_sends)
     finish(0, r0, c0)
     r1 = reduce_third(1, r1)
+    drain(early - 9)
     finish(1, r1, c1)
 
     for copy in all_sends:
@@ -510,6 +539,9 @@
     hbm = pl.BlockSpec(memory_space=pl.ANY)
     sem = pltpu.SemaphoreType.DMA
     scratch = [
+        pltpu.VMEM((MICRO, 8, 2048), BF16),
+        pltpu.VMEM((MICRO, 256), jnp.int32),
+        pltpu.VMEM((2, 128), F32),
         pltpu.VMEM((MICRO, 2, 8, 1024, 128), BF16),
         pltpu.VMEM((MICRO, N, N, 16, 1024), BF16),
         pltpu.VMEM((2, 2048, 256), BF16),
@@ -538,7 +570,7 @@
         pltpu.VMEM((MICRO, 16, 1024), BF16),
     ]
     scratch += [
-        sem((8 + W_CHUNKS,)),
+        sem((10 + W_CHUNKS,)),
         sem((16,)), sem((16,)),
         sem((MICRO, 2, 2, 3)), sem((MICRO, 2, 2, 3)),
         sem((MICRO, 3)), sem((MICRO, 3)),
@@ -549,7 +581,7 @@
     return pl.pallas_call(
         layer_kernel,
         out_shape=jax.ShapeDtypeStruct((MICRO, 8, 2048), BF16),
-        in_specs=[smem, vmem, hbm, vmem, hbm, hbm, vmem, hbm, hbm],
+        in_specs=[smem] + [hbm] * 8,
         out_specs=vmem,
         scratch_shapes=scratch,
         compiler_params=pltpu.CompilerParams(

time: 83.8 us -> 83.3 us (level)
  no operation moved by 1% of the time
where the time goes in v4:
time: 83.3 us; the launch traced here: 83.1 us
  Pallas kernels  81.6 us (98%)
  local copies, waits for them, and re-layouts  1.47 us (2%)
    pallas_call x1, Pallas kernels, shards(): pl.pallas_call(layer_kernel, out_shape=jax.ShapeDtypeStruct((MICRO, 8, 20...  81.6 us

profile of v4, /device:TPU:0, one launch (start us, length us, event | category | flops | bytes accessed | tf_op | source)
XLA Modules:
  0.0 83.1 jit_solution(3209797883076749739)
XLA Ops:
  0.0 81.6 %layer.1 = bf16[2,8,2048]{2,1,0:T(8,128)(2,1)} custom-call(s32[2,8]{1,0:T(2,128)} %len_ref.1, bf16[2,8,2048]{2,1,0:T(8,128)(2,1)} %query_in.1, bf16[2,8,2,1024,128]{4,3,2,1,0:T(8,128)(2,1)} %bitcast.8, s32[2,256]{1,0:T(2,128)} %rows_in.1, bf16[512,256]{1,0:T(8,128)(2,1)} %bitcast.10, bf16[2048,256]{1,0:T(8,128)(2,1)} %wo_ref.1, f32[2,128]{1,0:T(2,128)} %bitcast.11, ...), custom_call_target="tpu_custom_call" | custom-call | tf_op jit(solution)/shard_map/layer/pallas_call | solution.py:581
  81.6 1.5 %copy.12 = bf16[2,8,2048]{2,1,0:T(8,128)(2,1)} copy(bf16[2,8,2048]{2,1,0:T(8,128)(2,1)} %layer.1) | data formatting | bytes 131072

commit v5 on v4

--- a/solution.py
+++ b/solution.py
@@ -26,9 +26,9 @@
 
 
 def layer_kernel(
-    len_ref, query_in, cache_ref, rows_in, resid_ref, wo_ref, gain_in, wg_ref, wd_ref,
+    len_ref, query_ref, cache_ref, rows_in, resid_ref, wo_ref, gain_in, wg_ref, wd_ref,
     out_ref,
-    query_ref, rows_ref, gain_ref, kv, att_all, wo_all, resid_all, gain_all, w_raw, w_all, wd_all,
+    rows_ref, gain_ref, kv, att_all, wo_all, resid_all, gain_all, w_raw, w_all, wd_all,
     proj_send, proj_recv, gathered, stats, hid, pick,
     sums0, sums1, sums2, via0, via1, via2, in10, in11, in12, t10, t11, t12,
     in20, in21, in22, t20, t21, t22, in30, in31, in32,
@@ -81,8 +81,6 @@
         for copy in copies:
             copy.wait_recv()
 
-    query_load = local(query_in, query_ref, local_sem.at[8 + W_CHUNKS])
-
     barrier = pltpu.get_barrier_semaphore()
     for axis in range(3):
         for k in (1, 2, 3):
@@ -112,8 +110,6 @@
             raw_loads[chunk] = load_raw(chunk)
 
     def attend(m):
-        if m == 0:
-            query_load.wait()
         queries = query_ref[m].astype(F32)
         heads = queries.shape[1] // 128
         stacked = jnp.concatenate([queries[:, h * 128:(h + 1) * 128] for h in range(heads)], axis=0).astype(BF16)
@@ -514,11 +510,11 @@
     received([h1])
     middle = len(all_sends)
     r1 = down(1)
-    c1 = residual(1)
     drain(early)
     middle = middle - early
     r0 = reduce_second(0, r0)
     reduce_pass(1, r1)
+    c1 = residual(1)
     r0 = reduce_third(0, r0)
     r1 = reduce_second(1, r1)
     drain(middle)
@@ -539,7 +535,6 @@
     hbm = pl.BlockSpec(memory_space=pl.ANY)
     sem = pltpu.SemaphoreType.DMA
     scratch = [
-        pltpu.VMEM((MICRO, 8, 2048), BF16),
         pltpu.VMEM((MICRO, 256), jnp.int32),
         pltpu.VMEM((2, 128), F32),
         pltpu.VMEM((MICRO, 2, 8, 1024, 128), BF16),
@@ -581,7 +576,7 @@
     return pl.pallas_call(
         layer_kernel,
         out_shape=jax.ShapeDtypeStruct((MICRO, 8, 2048), BF16),
-        in_specs=[smem] + [hbm] * 8,
+        in_specs=[smem, vmem] + [hbm] * 7,
         out_specs=vmem,
         scratch_shapes=scratch,
         compiler_params=pltpu.CompilerParams(

time: 83.3 us -> 83.4 us (level)
  no operation moved by 1% of the time
where the time goes in v5:
time: 83.4 us; the launch traced here: 83.2 us
  Pallas kernels  81.8 us (98%)
  local copies, waits for them, and re-layouts  1.47 us (2%)
    pallas_call x1, Pallas kernels, shards(): pl.pallas_call(layer_kernel, out_shape=jax.ShapeDtypeStruct((MICRO, 8, 20...  81.8 us

profile of v5, /device:TPU:0, one launch (start us, length us, event | category | flops | bytes accessed | tf_op | source)
XLA Modules:
  0.0 83.2 jit_solution(340125916610052330)
XLA Ops:
  0.0 81.8 %layer.1 = bf16[2,8,2048]{2,1,0:T(8,128)(2,1)} custom-call(s32[2,8]{1,0:T(2,128)} %len_ref.1, bf16[2,8,2048]{2,1,0:T(8,128)(2,1)} %query_ref.1, bf16[2,8,2,1024,128]{4,3,2,1,0:T(8,128)(2,1)} %bitcast.8, s32[2,256]{1,0:T(2,128)} %rows_in.1, bf16[512,256]{1,0:T(8,128)(2,1)} %bitcast.10, bf16[2048,256]{1,0:T(8,128)(2,1)} %wo_ref.1, f32[2,128]{1,0:T(2,128)} %bitcast.11, ...), custom_call_target="tpu_custom_call" | custom-call | tf_op jit(solution)/shard_map/layer/pallas_call | solution.py:576
  81.8 1.5 %copy.12 = bf16[2,8,2048]{2,1,0:T(8,128)(2,1)} copy(bf16[2,8,2048]{2,1,0:T(8,128)(2,1)} %layer.1) | data formatting | bytes 131072
